TPU v7x, 32 devices: a whole 2x2x4 slice. The times are simulated.
32 devices in a mesh: scene: 4 (over z), rows: 8 (over y, x, core).
Axes of the slice: x: 2, y: 2, z: 4, core: 2. Of those that a mesh axis runs over, the one named last changes fastest.
Arguments:
- observations: float32 [512, 256, 512], P(('scene', 'rows')), may hold values from -100 to 100
- inverse_factor: float32 [512, 512], replicated, may hold values from -2 to 2, as said below
- tile_count: int32 [32], P(('scene', 'rows')), may hold values from 0 to 16
- tile_owner: int32 [512], P(('scene', 'rows')), may hold values from 0 to 3, as said below
- tile_slot: int32 [512], P(('scene', 'rows')), may hold values from 0 to 7
Outputs:
- orthonormal: float32 [256, 256, 512], P(('scene', 'rows'))
- factor: float32 [512, 512], replicated
Inputs may be any that keep to these rules, and one draw needn't show every extreme that they name: `tile_owner`: within each group (fixed rows index), every row-block owner's 8 slots are each named by exactly one live tile of that group; at most 4 live tiles of one device name the same owner, and in every group one device names every owner 4 times. `inverse_factor`: upper triangular with a positive diagonal.
All inputs are finite; a program needn't handle non-finite values.
Results may differ from a plain program's by a relative error of at most 0.0001.
Values sent between devices are 32-bit elements; how exact they have to be, the bound alone decides.
A program may use at most 128 MiB of HBM per device.

v0:
```python
import jax
import jax.numpy as jnp
from jax import lax
from jax.sharding import PartitionSpec as P

OWN_TILES = 8


def from_partner(shard, axis, bit):
    return lax.ppermute(shard, axis, [(i, i ^ 1 << bit) for i in range(lax.axis_size(axis))])


def gram_term(projected):
    return lax.dot_general(
        projected,
        projected,
        (((0,), (0,)), ((), ())),
        precision=lax.Precision.HIGHEST,
        preferred_element_type=jnp.float32,
    )


def shards(observations, inverse_factor, tile_count, tile_owner, tile_slot):
    scenes = lax.axis_size("scene")
    devices = scenes * lax.axis_size("rows")
    capacity = tile_owner.shape[0]
    pair_most = capacity // scenes
    tile_rows = observations.shape[1]
    column_count = observations.shape[2]
    position = jnp.arange(capacity, dtype=jnp.int32)
    is_live = position < tile_count[0]
    earlier = (
        (tile_owner[:, None] == tile_owner[None, :])
        & is_live[None, :]
        & (position[None, :] < position[:, None])
    )
    seat_rank = earlier.sum(1)
    target = jnp.where(is_live, tile_owner * pair_most + seat_rank, -1)
    selector = (target[None, :] == position[:, None]).astype(jnp.int32)
    filled = selector.sum(1) > 0
    chosen = (selector * position[None, :]).sum(1)
    slot_sent = (
        jnp.where(filled, (selector * tile_slot[None, :]).sum(1), -1)
        .astype(jnp.float32)
        .reshape(scenes, pair_most)
    )
    keep_mask = filled.astype(jnp.float32)[:, None, None]
    outgoing = jnp.take(observations, chosen, axis=0) * keep_mask
    received, slot_ids = (
        lax.all_to_all(
            outgoing.reshape(scenes, pair_most, tile_rows, column_count),
            "scene",
            split_axis=0,
            concat_axis=0,
            tiled=True,
        ),
        lax.all_to_all(slot_sent, "scene", split_axis=0, concat_axis=0, tiled=True),
    )
    flat_tiles = received.reshape(capacity, tile_rows, column_count)
    slot_flat = slot_ids.reshape(capacity).astype(jnp.int32)
    matches = (slot_flat[None, :] == jnp.arange(OWN_TILES, dtype=jnp.int32)[:, None]).astype(
        jnp.int32
    )
    order_idx = (matches * position[None, :]).sum(1)
    row_block = jnp.take(flat_tiles, order_idx, axis=0).reshape(-1, column_count)
    projected = jnp.dot(
        row_block,
        inverse_factor,
        precision=lax.Precision.HIGHEST,
        preferred_element_type=jnp.float32,
    )
    partial_value = gram_term(projected)
    gram_sum = partial_value
    for bit_index in range(devices.bit_length() - 1):
        gram_sum = gram_sum + from_partner(gram_sum, ("scene", "rows"), bit_index)
    weight = gram_sum / (devices * OWN_TILES * tile_rows)
    lower_factor = jnp.linalg.cholesky(weight)
    identity = jnp.eye(column_count, dtype=jnp.float32)
    inv_upper = jax.scipy.linalg.solve_triangular(lower_factor, identity, lower=True).T
    orthonormal = jnp.dot(
        projected, inv_upper, precision=lax.Precision.HIGHEST, preferred_element_type=jnp.float32
    )
    return (orthonormal.reshape(OWN_TILES, tile_rows, column_count), lower_factor.T)


def solution(mesh):
    in_specs = (
        P(("scene", "rows"), None, None),
        P(),
        P(("scene", "rows")),
        P(("scene", "rows")),
        P(("scene", "rows")),
    )
    out_specs = (P(("scene", "rows"), None, None), P())
    return jax.shard_map(shards, mesh=mesh, in_specs=in_specs, out_specs=out_specs, check_vma=False)
```

profile of v0, /device:TPU:0, one launch (start us, length us, event | category | flops | bytes accessed | tf_op | source)
XLA Modules:
  0.0 523.6 jit_solution(12950500984363263968)
XLA Ops:
  1.4 0.9 convert_reduce_fusion.1
  2.3 0.7 add_select_fusion
  3.0 0.8 select_reduce_fusion.5
  3.8 0.7 convert_element_type.51
  4.5 6.3 %all-to-all-start = ((f32[4,1,4]{2,1,0:T(1,128)}), f32[4,1,4]{2,1,0:T(1,128)S(1)}, u32[]{:S(2)}, u32[]{:S(2)}) async-start(f32[4,1,4]{2,1,0:T(1,128)} %bitcast.1), calls=%async_computation | async-start | bytes 4096 | tf_op jit(solution)/shard_map/all_to_all | solution.py:57
  11.0 7.7 %gather_fusion = f32[16,256,512]{2,1,0:T(8,128)} fusion(f32[16,256,512]{2,1,0:T(8,128)} %param.5, s32[1024]{0:T(1024)S(1)} %pad_clamp_fusion.1), kind=kCustom, calls=%fused_computation | custom fusion | bytes 16777280 | tf_op jit(solution)/shard_map/jit(_take)/gather | solution.py:48
  18.6 7.8 %select_multiply_fusion = f32[4,4,256,512]{3,2,1,0:T(8,128)} fusion(f32[4,4,256,512]{3,2,1,0:T(8,128)} %bitcast.72, f32[4,4]{1,0:T(4,128)S(1)} %reshape.173, pred[4,4]{1,0:T(4,128)(4,1)S(1)} %compare_and_fusion), kind=kLoop, calls=%fused_computation.4 | loop fusion | flops 4194304 | bytes 16777296 | tf_op jit(solution)/shard_map/mul | solution.py:48
  26.5 5.7 %all-to-all-start.1 = ((f32[4,4,256,512]{3,2,1,0:T(8,128)}), f32[4,4,256,512]{3,2,1,0:T(8,128)}, u32[]{:S(2)}, u32[]{:S(2)}) async-start(f32[4,4,256,512]{3,2,1,0:T(8,128)} %select_multiply_fusion), calls=%async_computation.1 | async-start | bytes 16777216 | tf_op jit(solution)/shard_map/all_to_all | solution.py:50
  32.6 182.7 %all-to-all-done.1 = f32[4,4,256,512]{3,2,1,0:T(8,128)} async-done(((f32[4,4,256,512]{3,2,1,0:T(8,128)}), f32[4,4,256,512]{3,2,1,0:T(8,128)}, u32[]{:S(2)}, u32[]{:S(2)}) %all-to-all-start.1) | async-done | bytes 8388640 | tf_op jit(solution)/shard_map/all_to_all | solution.py:50
  215.3 6.2 %gather_fusion.1 = f32[8,256,512]{2,1,0:T(8,128)} fusion(f32[16,256,512]{2,1,0:T(8,128)} %bitcast.5, s32[1024]{0:T(1024)S(1)} %pad_clamp_fusion), kind=kCustom, calls=%fused_computation.1 | custom fusion | bytes 8388640 | tf_op jit(solution)/shard_map/jit(_take)/gather | solution.py:65
  221.5 2.9 bitcast_select_fusion
  224.4 7.5 %fusion.47 = f32[2048,512]{1,0:T(8,128)S(1)} fusion(f32[2048,512]{1,0:T(8,128)S(1)} %bitcast_select_fusion, f32[512,512]{1,0:T(8,128)S(1)} %copy-done), kind=kOutput, calls=%fused_computation.109 | convolution fusion | flops 6442450944 | bytes 9437184 | tf_op jit(solution)/shard_map/dot_general | solution.py:66
  231.9 7.2 %fusion.48 = f32[512,512]{0,1:T(8,128)S(1)} fusion(f32[2048,512]{1,0:T(8,128)S(1)} %fusion.47), kind=kOutput, calls=%fused_computation.110 | convolution fusion | flops 6442450944 | bytes 5242880 | tf_op jit(solution)/shard_map/dot_general | solution.py:14
  239.3 2.6 collective-permute-done
  241.9 0.2 add.95
  242.1 1.6 collective-permute-start.1
  243.7 23.7 %collective-permute-done.1 = f32[512,512]{0,1:T(8,128)S(1)} collective-permute-done((f32[512,512]{0,1:T(8,128)S(1)}, f32[512,512]{0,1:T(8,128)S(1)}, u32[]{:S(2)}, u32[]{:S(2)}) %collective-permute-start.1) | collective-permute-done | bytes 1048608 | tf_op jit(solution)/shard_map/ppermute | solution.py:10
  267.4 0.2 add.96
  267.6 1.6 collective-permute-start.2
  269.2 22.8 %collective-permute-done.2 = f32[512,512]{0,1:T(8,128)S(1)} collective-permute-done((f32[512,512]{0,1:T(8,128)S(1)}, f32[512,512]{0,1:T(8,128)S(1)}, u32[]{:S(2)}, u32[]{:S(2)}) %collective-permute-start.2) | collective-permute-done | bytes 1048608 | tf_op jit(solution)/shard_map/ppermute | solution.py:10
  292.1 0.2 add.97
  292.3 23.4 %collective-permute-done.3 = f32[512,512]{0,1:T(8,128)S(1)} collective-permute-done((f32[512,512]{0,1:T(8,128)S(1)}, f32[512,512]{0,1:T(8,128)S(1)}, u32[]{:S(2)}, u32[]{:S(2)}) %collective-permute-start.3) | collective-permute-done | bytes 1048608 | tf_op jit(solution)/shard_map/ppermute | solution.py:10
  315.8 0.2 add.98
  316.0 0.4 collective-permute-start.4
  316.6 45.5 %collective-permute-done.4 = f32[512,512]{0,1:T(8,128)} collective-permute-done((f32[512,512]{0,1:T(8,128)S(1)}, f32[512,512]{0,1:T(8,128)}, u32[]{:S(2)}, u32[]{:S(2)}) %collective-permute-start.4) | collective-permute-done | bytes 1048608 | tf_op jit(solution)/shard_map/ppermute | solution.py:10
  362.1 1.4 add_multiply_fusion
  363.5 0.3 copy.19
  363.9 0.2 fusion.8
  364.1 1.0 copy-done.4
  365.1 11.7 %cholesky.104 = f32[128,128]{1,0:T(8,128)S(1)} custom-call(f32[128,128]{1,0:T(8,128)S(1)} %cholesky.266), custom_call_target="Cholesky" | custom-call | tf_op jit(solution)/shard_map/jit(cholesky)/cholesky | solution.py:77
  376.9 9.8 %custom-call.31 = f32[1,128,128]{1,2,0:T(8,128)S(1)} custom-call(f32[1,128,128]{2,1,0:T(8,128)S(1)} %get-tuple-element.40), custom_call_target="InvertDiagBlocksLowerTriangular" | custom-call | tf_op jit(solution)/shard_map/jit(cholesky)/cholesky | solution.py:77
  386.8 1.2 constant_dynamic-update-slice_fusion.3
  388.0 1.3 convolution_subtract_fusion.3
  389.3 11.9 %cholesky.217 = f32[128,128]{1,0:T(8,128)S(1)} custom-call(f32[128,128]{1,0:T(8,128)S(1)} %cholesky.270), custom_call_target="Cholesky" | custom-call | tf_op jit(solution)/shard_map/jit(cholesky)/cholesky | solution.py:77
  401.2 9.8 %custom-call.32 = f32[1,128,128]{1,2,0:T(8,128)S(1)} custom-call(f32[1,128,128]{2,1,0:T(8,128)S(1)} %get-tuple-element.37), custom_call_target="InvertDiagBlocksLowerTriangular" | custom-call | tf_op jit(solution)/shard_map/jit(cholesky)/cholesky | solution.py:77
  411.0 0.3 convolution_dynamic-update-slice_fusion
  411.3 1.3 convolution_subtract_fusion.4
  412.6 11.7 %cholesky.238 = f32[128,128]{1,0:T(8,128)S(1)} custom-call(f32[128,128]{1,0:T(8,128)S(1)} %cholesky.275), custom_call_target="Cholesky" | custom-call | tf_op jit(solution)/shard_map/jit(cholesky)/cholesky | solution.py:77
  424.4 0.7 compare_reduce_fusion.1
  425.1 9.8 %custom-call.33 = f32[1,128,128]{1,2,0:T(8,128)S(1)} custom-call(f32[1,128,128]{2,1,0:T(8,128)S(1)} %get-tuple-element.34), custom_call_target="InvertDiagBlocksLowerTriangular" | custom-call | tf_op jit(solution)/shard_map/jit(cholesky)/cholesky | solution.py:77
  435.1 1.2 convolution_subtract_fusion.5
  436.3 11.9 %cholesky.255 = f32[128,128]{1,0:T(8,128)S(1)} custom-call(f32[128,128]{1,0:T(8,128)S(1)} %convolution_subtract_fusion.5), custom_call_target="Cholesky" | custom-call | tf_op jit(solution)/shard_map/jit(cholesky)/cholesky | solution.py:77
  448.3 0.6 compare_reduce_fusion
  449.0 0.7 compare_reduce_fusion.2
  452.2 1.2 fusion.10
  453.4 14.1 %while.1 = (s32[]{:T(128)}, f32[512,512]{1,0:T(8,128)}, s32[4,2]{0,1:T(2,128)S(1)}, f32[4,128,128]{2,1,0:T(8,128)}, s32[]{:T(128)}) while((s32[]{:T(128)}, f32[512,512]{1,0:T(8,128)}, s32[4,2]{0,1:T(2,128)S(1)}, f32[4,128,128]{2,1,0:T(8,128)}, s32[]{:T(128)}) %tuple.37), condition=%wide.while_cond, body=%wide.while_body.sunk | while | flops 2 | bytes 132705 | solution.py:79
  453.5 0.6 fusion.60
  454.1 2.9 bitcast_dynamic-update-slice_fusion.2
  457.0 0.6 fusion.60
  457.6 2.9 bitcast_dynamic-update-slice_fusion.2
  460.6 0.6 fusion.60
  461.2 2.9 bitcast_dynamic-update-slice_fusion.2
  464.1 0.6 fusion.60
  464.7 2.8 bitcast_dynamic-update-slice_fusion.2
  467.5 40.1 %custom-call.34 = f32[4,128,128]{1,2,0:T(8,128)S(1)} custom-call(f32[4,128,128]{2,1,0:T(8,128)} %get-tuple-element.9), custom_call_target="InvertDiagBlocksLowerTriangular" | custom-call | tf_op jit(solution)/shard_map/jit(_solve_triangular)/triangular_solve | solution.py:79
  507.7 0.3 fusion.21
  508.0 1.4 convolution_subtract_fusion.1
  509.4 0.4 fusion.33
  509.8 1.3 convolution_subtract_fusion
  511.1 0.4 fusion.31
  511.6 1.6 convolution_subtract_fusion.2
  513.1 0.4 fusion.30
  513.6 8.3 %fusion = f32[2048,512]{1,0:T(8,128)} fusion(f32[2048,512]{1,0:T(8,128)S(1)} %copy-done.3, f32[128,512]{1,0:T(8,128)S(1)} %fusion.30, f32[128,512]{1,0:T(8,128)S(1)} %fusion.31, f32[128,512]{1,0:T(8,128)S(1)} %fusion.33, f32[128,512]{1,0:T(8,128)S(1)} %fusion.21), kind=kOutput, calls=%fused_computation.14 | convolution fusion | flops 6443237376 | bytes 9437184 | tf_op jit(solution)/shard_map/dot_general | solution.py:80
  521.9 1.3 copy.20
  (46 shorter events, 1.7 us)
Async XLA Ops:
  0.6 223.8 %copy-start = (f32[512,512]{1,0:T(8,128)S(1)}, f32[512,512]{1,0:T(8,128)}, u32[]{:S(2)}) copy-start(f32[512,512]{1,0:T(8,128)} %param.6) | copy-start | bytes 3145732
  4.5 22.0 %all-to-all-start = ((f32[4,1,4]{2,1,0:T(1,128)}), f32[4,1,4]{2,1,0:T(1,128)S(1)}, u32[]{:S(2)}, u32[]{:S(2)}) async-start(f32[4,1,4]{2,1,0:T(1,128)} %bitcast.1), calls=%async_computation | async-start | bytes 4096 | tf_op jit(solution)/shard_map/all_to_all | solution.py:57
  26.5 188.8 %all-to-all-start.1 = ((f32[4,4,256,512]{3,2,1,0:T(8,128)}), f32[4,4,256,512]{3,2,1,0:T(8,128)}, u32[]{:S(2)}, u32[]{:S(2)}) async-start(f32[4,4,256,512]{3,2,1,0:T(8,128)} %select_multiply_fusion), calls=%async_computation.1 | async-start | bytes 16777216 | tf_op jit(solution)/shard_map/all_to_all | solution.py:50
  231.9 7.3 %copy-start.2 = (f32[2048,512]{1,0:T(8,128)}, f32[2048,512]{1,0:T(8,128)S(1)}, u32[]{:S(2)}) copy-start(f32[2048,512]{1,0:T(8,128)S(1)} %fusion.47) | copy-start | bytes 12582916
  239.2 2.7 collective-permute-start
  242.1 25.3 %collective-permute-start.1 = (f32[512,512]{0,1:T(8,128)S(1)}, f32[512,512]{0,1:T(8,128)S(1)}, u32[]{:S(2)}, u32[]{:S(2)}) collective-permute-start(f32[512,512]{0,1:T(8,128)S(1)} %add.95), channel_id=1, source_target_pairs={{0,2},{1,3},{2,0},{3,1},{4,6},{5,7},{6,4},{7,5},{8,10},{9,11},{10,... | collective-permute-start | bytes 3145736 | tf_op jit(solution)/shard_map/ppermute | solution.py:10
  267.6 24.4 %collective-permute-start.2 = (f32[512,512]{0,1:T(8,128)S(1)}, f32[512,512]{0,1:T(8,128)S(1)}, u32[]{:S(2)}, u32[]{:S(2)}) collective-permute-start(f32[512,512]{0,1:T(8,128)S(1)} %add.96), channel_id=1, source_target_pairs={{0,4},{1,5},{2,6},{3,7},{4,0},{5,1},{6,2},{7,3},{8,12},{9,13},{10,... | collective-permute-start | bytes 3145736 | tf_op jit(solution)/shard_map/ppermute | solution.py:10
  292.3 23.5 %collective-permute-start.3 = (f32[512,512]{0,1:T(8,128)S(1)}, f32[512,512]{0,1:T(8,128)S(1)}, u32[]{:S(2)}, u32[]{:S(2)}) collective-permute-start(f32[512,512]{0,1:T(8,128)S(1)} %add.97), channel_id=1, source_target_pairs={{0,8},{1,9},{2,10},{3,11},{4,12},{5,13},{6,14},{7,15},{8,0},{9,1},... | collective-permute-start | bytes 3145736 | tf_op jit(solution)/shard_map/ppermute | solution.py:10
  316.0 46.1 %collective-permute-start.4 = (f32[512,512]{0,1:T(8,128)S(1)}, f32[512,512]{0,1:T(8,128)}, u32[]{:S(2)}, u32[]{:S(2)}) collective-permute-start(f32[512,512]{0,1:T(8,128)S(1)} %add.98), channel_id=1, source_target_pairs={{0,16},{1,17},{2,18},{3,19},{4,20},{5,21},{6,22},{7,23},{8,24},{9,... | collective-permute-start | bytes 3145736 | tf_op jit(solution)/shard_map/ppermute | solution.py:10
  364.1 1.0 copy-start.4
  507.6 5.9 %copy-start.3 = (f32[2048,512]{1,0:T(8,128)S(1)}, f32[2048,512]{1,0:T(8,128)}, u32[]{:S(2)}) copy-start(f32[2048,512]{1,0:T(8,128)} %copy-done.2) | copy-start | bytes 12582916
  513.6 9.6 %copy-start.1 = (f32[512,512]{1,0:T(8,128)S(1)}, f32[512,512]{1,0:T(8,128)}, u32[]{:S(2)}) copy-start(f32[512,512]{1,0:T(8,128)} %param.6) | copy-start | bytes 3145732
where the time goes:
time: 527 us; the launch traced here: 524 us
  waiting for transfers between devices  301 us (57%)
  other arithmetic  136 us (26%)
  matrix products  34.3 us (7%)
  local copies, waits for them, and re-layouts  31.8 us (6%)
  starting transfers between devices  15.7 us (3%)
    all_to_all x1, waiting for transfers between devices, shards(): lax.all_to_all(outgoing.reshape(scenes, pair_most, tile_rows, column_coun...  183 us
    ppermute x5, waiting for transfers between devices, from_partner(): lax.ppermute(shard, axis, [(i, i ^ 1 << bit) for i in range(lax.axis_size...  118 us
    another operation x14, other arithmetic, shards(): lower_factor = jnp.linalg.cholesky(weight)  78.9 us
    another operation x2, other arithmetic, shards(): jax.scipy.linalg.solve_triangular(lower_factor, identity, lower=True)  40.1 us
    another operation x12, local copies, waits for them, and re-layouts  14.1 us
  transfers between devices with their start and end apart: 7, of which 6 were waited for; matrix products, arithmetic and copies ran while one was open for 3% of the time, Pallas kernels for 0%

commit v1 on v0

v1 whole, which is shorter than its diff:
```python
import functools

import jax
import jax.numpy as jnp
from jax import lax
from jax.experimental import pallas as pl
from jax.experimental.pallas import tpu as pltpu
from jax.sharding import PartitionSpec as P

OWN_TILES = 8
NB = 128
HALF = 256


def split(x):
    hi = x.astype(jnp.bfloat16)
    return hi, (x - hi.astype(jnp.float32)).astype(jnp.bfloat16)


def mm(a, b):
    return jnp.dot(a, b, preferred_element_type=jnp.float32)


def upper_product(x, uh, ul):
    xh, xl = split(x)
    left = slice(0, HALF)
    right = slice(HALF, None)
    a = mm(xh[:, left], uh[left, left]) + (mm(xh[:, left], ul[left, left]) + mm(xl[:, left], uh[left, left]))
    b = mm(xh, uh[:, right]) + (mm(xh, ul[:, right]) + mm(xl, uh[:, right]))
    return a, b


def copy_kernel(index_ref, x_ref, o_ref):
    o_ref[...] = x_ref[...]


def gather_tiles(index, tiles):
    block = (1,) + tiles.shape[1:]
    return pl.pallas_call(
        copy_kernel,
        grid_spec=pltpu.PrefetchScalarGridSpec(
            num_scalar_prefetch=1,
            grid=(index.shape[0],),
            in_specs=[pl.BlockSpec(block, lambda i, idx: (idx[i], 0, 0))],
            out_specs=pl.BlockSpec(block, lambda i, idx: (i, 0, 0)),
        ),
        out_shape=jax.ShapeDtypeStruct((index.shape[0],) + tiles.shape[1:], tiles.dtype),
        name="gather_tiles",
    )(index, tiles)


def gram_kernel(count_ref, x_ref, r_ref, g_ref, rh, rl, low, cross):
    i = pl.program_id(0)

    @pl.when(i == 0)
    def _():
        h, l = split(r_ref[...])
        rh[...] = h
        rl[...] = l
        low[...] = jnp.zeros_like(low)
        cross[...] = jnp.zeros_like(cross)

    @pl.when(i < count_ref[0])
    def _():
        a, b = upper_product(x_ref[0], rh[...], rl[...])
        ah, al = split(a)
        bh, bl = split(b)
        at = ah.T
        bt = bh.T
        low[:HALF, :HALF] += mm(at, ah)
        low[HALF:, :HALF] += mm(bt, ah)
        low[HALF:, HALF:] += mm(bt, bh)
        cross[:HALF, :HALF] += mm(at, al)
        cross[:HALF, HALF:] += mm(at, bl)
        cross[HALF:, :HALF] += mm(bt, al)
        cross[HALF:, HALF:] += mm(bt, bl)

    @pl.when(i == pl.num_programs(0) - 1)
    def _():
        c = cross[...]
        g_ref[...] = c + c.T
        g_ref[:HALF, :HALF] += low[:HALF, :HALF]
        g_ref[HALF:, HALF:] += low[HALF:, HALF:]
        corner = low[HALF:, :HALF]
        g_ref[HALF:, :HALF] += corner
        g_ref[:HALF, HALF:] += corner.T


def local_gram(count, tiles, inverse_factor):
    capacity, rows, n = tiles.shape
    return pl.pallas_call(
        gram_kernel,
        grid_spec=pltpu.PrefetchScalarGridSpec(
            num_scalar_prefetch=1,
            grid=(capacity,),
            in_specs=[
                pl.BlockSpec(
                    (1, rows, n), lambda i, c: (jnp.minimum(i, jnp.maximum(c[0] - 1, 0)), 0, 0)
                ),
                pl.BlockSpec((n, n), lambda i, c: (0, 0)),
            ],
            out_specs=pl.BlockSpec((n, n), lambda i, c: (0, 0)),
            scratch_shapes=[
                pltpu.VMEM((n, n), jnp.bfloat16),
                pltpu.VMEM((n, n), jnp.bfloat16),
                pltpu.VMEM((n, n), jnp.float32),
                pltpu.VMEM((n, n), jnp.float32),
            ],
        ),
        out_shape=jax.ShapeDtypeStruct((n, n), jnp.float32),
        compiler_params=pltpu.CompilerParams(vmem_limit_bytes=40 * 2**20),
        cost_estimate=pl.CostEstimate(
            flops=8 * capacity * rows * n * n, bytes_accessed=4 * capacity * rows * n, transcendentals=0
        ),
        name="local_gram",
    )(count, tiles, inverse_factor)


def eliminate(block):
    lane = lax.broadcasted_iota(jnp.int32, (8, NB), 1)
    sub = lax.broadcasted_iota(jnp.int32, (8, 1), 0)
    groups = [block[8 * g : 8 * g + 8, :] for g in range(NB // 8)]
    for j in range(NB - 1):
        first, r = divmod(j, 8)
        row = groups[first][r : r + 1, :]
        inverse = 1.0 / row[:, j : j + 1]
        here = lane == j
        row = jnp.where(here[:1], 1.0, row)
        for g in range(first if r < 7 else first + 1, NB // 8):
            c = groups[g]
            coef = c[:, j : j + 1] * inverse
            if g == first:
                live = sub > r
                coef = jnp.where(live, coef, 0.0)
                base = jnp.where(here & live, 0.0, c)
            else:
                base = jnp.where(here, 0.0, c)
            groups[g] = base - coef * row
    return jnp.concatenate(groups, axis=0)


def hdot(a, b, dims=((1,), (0,))):
    return lax.dot_general(
        a, b, (dims, ((), ())), precision=lax.Precision.HIGHEST, preferred_element_type=jnp.float32
    )


def factor_kernel(rows_all, g_ref, r_ref, u_ref, mh_ref, ml_ref, work):
    n = g_ref.shape[0]
    work[:, :n] = g_ref[...] / rows_all
    work[:, n:] = (
        lax.broadcasted_iota(jnp.int32, (n, n), 0) == lax.broadcasted_iota(jnp.int32, (n, n), 1)
    ).astype(jnp.float32)

    def step(k, carry):
        at = pl.multiple_of(k * NB, NB)
        here = pl.ds(at, NB)
        done = eliminate(work[here, here])
        i = lax.broadcasted_iota(jnp.int32, (NB, NB), 0)
        j = lax.broadcasted_iota(jnp.int32, (NB, NB), 1)
        scale = lax.rsqrt(jnp.sum(jnp.where(i == j, done, 0.0), axis=1, keepdims=True))
        inverse = jnp.where(i > j, done, jnp.where(i == j, 1.0, 0.0)) * scale
        panel = hdot(inverse, work[here, :])
        work[here, :] = panel
        work[here, here] = jnp.where(i <= j, done, 0.0) * scale
        column = lax.broadcasted_iota(jnp.int32, (NB, n), 1)
        coef = jnp.where(column >= at + NB, panel[:, :n], 0.0)

        @pl.when(k < n // NB - 1)
        def _():
            work[...] -= hdot(coef, panel, ((0,), (0,)))

        return carry

    lax.fori_loop(0, n // NB, step, 0)
    i = lax.broadcasted_iota(jnp.int32, (n, n), 0)
    j = lax.broadcasted_iota(jnp.int32, (n, n), 1)
    u_ref[...] = jnp.where(i <= j, work[:, :n], 0.0)
    m = hdot(r_ref[...], work[:, n:], ((1,), (1,)))
    h, l = split(m)
    mh_ref[...] = h
    ml_ref[...] = l


def factorise(gram, inverse_factor, rows_all):
    n = gram.shape[0]
    return pl.pallas_call(
        functools.partial(factor_kernel, rows_all),
        out_shape=[
            jax.ShapeDtypeStruct((n, n), jnp.float32),
            jax.ShapeDtypeStruct((n, n), jnp.bfloat16),
            jax.ShapeDtypeStruct((n, n), jnp.bfloat16),
        ],
        in_specs=[pl.BlockSpec(memory_space=pltpu.VMEM)] * 2,
        out_specs=[pl.BlockSpec(memory_space=pltpu.VMEM)] * 3,
        scratch_shapes=[pltpu.VMEM((n, 2 * n), jnp.float32)],
        compiler_params=pltpu.CompilerParams(vmem_limit_bytes=40 * 2**20),
        cost_estimate=pl.CostEstimate(flops=40 * n**3, bytes_accessed=16 * n * n, transcendentals=0),
        name="factorise",
    )(gram, inverse_factor)


def last_kernel(index_ref, x_ref, mh_ref, ml_ref, o_ref):
    a, b = upper_product(x_ref[0], mh_ref[...], ml_ref[...])
    o_ref[0, :, :HALF] = a
    o_ref[0, :, HALF:] = b


def last_product(index, tiles, mh, ml):
    rows, n = tiles.shape[1:]
    whole = pl.BlockSpec((n, n), lambda i, idx: (0, 0))
    return pl.pallas_call(
        last_kernel,
        grid_spec=pltpu.PrefetchScalarGridSpec(
            num_scalar_prefetch=1,
            grid=(OWN_TILES,),
            in_specs=[pl.BlockSpec((1, rows, n), lambda i, idx: (idx[i], 0, 0)), whole, whole],
            out_specs=pl.BlockSpec((1, rows, n), lambda i, idx: (i, 0, 0)),
        ),
        out_shape=jax.ShapeDtypeStruct((OWN_TILES, rows, n), jnp.float32),
        compiler_params=pltpu.CompilerParams(vmem_limit_bytes=32 * 2**20),
        name="last_product",
    )(index, tiles, mh, ml)


def seats(owner, count, scenes):
    capacity = owner.shape[0]
    position = jnp.arange(capacity, dtype=jnp.int32)
    is_live = position < count
    earlier = (owner[:, None] == owner[None, :]) & is_live[None, :] & (position[None, :] < position[:, None])
    rank = earlier.astype(jnp.int32).sum(1)
    return is_live, rank


def shards(observations, inverse_factor, tile_count, tile_owner, tile_slot):
    scenes = lax.axis_size("scene")
    devices = scenes * lax.axis_size("rows")
    capacity = tile_owner.shape[0]
    pair_most = capacity // scenes
    tile_rows, n = observations.shape[1:]
    position = jnp.arange(capacity, dtype=jnp.int32)

    is_live, rank = seats(tile_owner, tile_count[0], scenes)
    target = jnp.where(is_live, tile_owner * pair_most + rank, -1)
    selector = (target[None, :] == position[:, None]).astype(jnp.int32)
    chosen = (selector * position[None, :]).sum(1)
    outgoing = gather_tiles(chosen, observations)
    received = lax.all_to_all(
        outgoing.reshape(scenes, pair_most, tile_rows, n), "scene", split_axis=0, concat_axis=0, tiled=True
    ).reshape(capacity, tile_rows, n)

    me = lax.axis_index("scene")
    note = jnp.where(is_live, (tile_owner * pair_most + rank) * OWN_TILES + tile_slot, -1)
    notes = lax.all_gather(note, "scene")
    seat = notes // OWN_TILES
    mine = (notes >= 0) & (seat // pair_most == me)
    place = jnp.arange(scenes, dtype=jnp.int32)[:, None] * pair_most + seat % pair_most
    match = mine[None] & ((notes % OWN_TILES)[None] == jnp.arange(OWN_TILES, dtype=jnp.int32)[:, None, None])
    order = jnp.where(match, place[None], 0).sum((1, 2))

    gram = lax.psum(local_gram(tile_count, observations, inverse_factor), ("scene", "rows"))
    factor, mh, ml = factorise(gram, inverse_factor, devices * OWN_TILES * tile_rows)
    return last_product(order, received, mh, ml), factor


def solution(mesh):
    in_specs = (
        P(("scene", "rows"), None, None),
        P(),
        P(("scene", "rows")),
        P(("scene", "rows")),
        P(("scene", "rows")),
    )
    out_specs = (P(("scene", "rows"), None, None), P())
    return jax.shard_map(shards, mesh=mesh, in_specs=in_specs, out_specs=out_specs, check_vma=False)
```

time: 527 us -> 394 us (0.75)
  waiting for transfers between devices: 301 us -> 102 us
  blocking collectives: 0 us -> 183 us
  other arithmetic: 136 us -> 2.53 us
  Pallas kernels: 0 us -> 73 us
  matrix products: 34.3 us -> 0 us
  local copies, waits for them, and re-layouts: 31.8 us -> 5.93 us
  between operations: 4.71 us -> 15.4 us
  starting transfers between devices: 15.7 us -> 10.3 us
    unnamed x0 -> x1, blocking collectives: none -> 183 us
    all_to_all x2 -> x1, waiting for transfers between devices: 183 us -> 0.01 us  [shards(): lax.all_to_all(outgoing.reshape(scenes, pair_most, tile_rows, n), 'scene'...]
    another operation x16 -> x0, other arithmetic: 119 us -> none  [the longest x14 78.9 us: shards(): lower_factor = jnp.linalg.cholesky(weight)]
    ppermute x5 -> x0, waiting for transfers between devices: 118 us -> none  [from_partner(): lax.ppermute(shard, axis, [(i, i ^ 1 << bit) for i in range(lax.axis_size...]
    psum x0 -> x1, waiting for transfers between devices: none -> 102 us  [shards(): lax.psum(local_gram(tile_count, observations, inverse_factor), ('scene',...]
    pallas_call x0 -> x4, Pallas kernels: none -> 73 us  [the longest x1 53.4 us: factorise(): pl.pallas_call(functools.partial(factor_kernel, rows_all), out_shape=[jax...]
    dot_general x3 -> x0, matrix products: 23 us -> none  [the longest x1 8.29 us: shards(): jnp.dot(projected, inv_upper, precision=lax.Precision.HIGHEST, preferred_...]
    another operation x17 -> x0, local copies, waits for them, and re-layouts: 14.2 us -> none
  transfers between devices with their start and end apart: 7 -> 2, of which waited for: 6 -> 1; matrix products, arithmetic and copies ran while one was open for 3% -> 0% of each run, Pallas kernels for 0% -> 14%
where the time goes in v1:
time: 394 us; the launch traced here: 393 us
  blocking collectives  183 us (46%)
  waiting for transfers between devices  102 us (26%)
  Pallas kernels  73 us (19%)
  between operations  15.4 us (4%)
  starting transfers between devices  10.3 us (3%)
  local copies, waits for them, and re-layouts  5.93 us (2%)
    unnamed x1, blocking collectives  183 us
    psum x1, waiting for transfers between devices, shards(): lax.psum(local_gram(tile_count, observations, inverse_factor), ('scene',...  102 us
    pallas_call x1, Pallas kernels, factorise(): pl.pallas_call(functools.partial(factor_kernel, rows_all), out_shape=[jax...  53.4 us
    all_to_all x1, starting transfers between devices, shards(): lax.all_to_all(outgoing.reshape(scenes, pair_most, tile_rows, n), 'scene'...  10.3 us
    pallas_call x1, Pallas kernels, last_product(): pl.pallas_call(last_kernel, grid_spec=pltpu.PrefetchScalarGridSpec(num_sc...  8.79 us
    pallas_call x1, Pallas kernels, gather_tiles(): pl.pallas_call(copy_kernel, grid_spec=pltpu.PrefetchScalarGridSpec(num_sc...  8.71 us
  transfers between devices with their start and end apart: 2, of which 1 were waited for; matrix products, arithmetic and copies ran while one was open for 0% of the time, Pallas kernels for 14%

profile of v1, /device:TPU:0, one launch (start us, length us, event | category | flops | bytes accessed | tf_op | source)
XLA Modules:
  0.0 392.8 jit_solution(9122908029126390393)
XLA Ops:
  7.8 0.9 convert_reduce_fusion
  8.7 1.2 dynamic-slice
  10.7 0.8 broadcast_select_fusion
  11.4 0.6 select_reduce_fusion.1.index_ref
  12.0 8.7 %gather_tiles.1 = f32[16,256,512]{2,1,0:T(8,128)} custom-call(s32[16]{0:T(128)} %select_reduce_fusion.1.index_ref, f32[16,256,512]{2,1,0:T(8,128)} %x_ref.3), custom_call_target="tpu_custom_call" | custom-call | tf_op jit(solution)/shard_map/gather_tiles/pallas_call | solution.py:39
  20.8 0.0 copy-start.1
  20.8 10.3 %all-to-all-start = ((f32[4,4,256,512]{3,2,1,0:T(8,128)}), f32[4,4,256,512]{3,2,1,0:T(8,128)}, u32[]{:S(2)}, u32[]{:S(2)}) async-start(f32[4,4,256,512]{3,2,1,0:T(8,128)} %bitcast.6), calls=%async_computation | async-start | bytes 16777216 | tf_op jit(solution)/shard_map/all_to_all | solution.py:248
  31.1 0.0 all-reduce.3.cloned.1.call-start
  31.1 0.0 copy-done.1
  31.1 0.0 copy-start
  31.1 3.4 copy-done
  34.4 2.1 local_gram.1
  36.6 0.0 all-reduce.3.cloned.1.call-update
  36.6 183.3 %all-reduce = s32[64]{0:T(128)S(1)} all-reduce(s32[64]{0:T(128)S(1)} %get-tuple-element.11), channel_id=2, replica_groups=mesh['scene'=4,'rows'=8] {'scene'}, use_global_device_ids=true, to_apply=%add | all-reduce | flops 64 | bytes 512
  219.9 0.1 reshape.27
  220.0 0.1 add_select_fusion.1
  220.1 0.1 select_reduce_fusion.index_ref
  220.2 102.4 %all-reduce.3.cloned.1.call-done.g_ref = f32[512,512]{1,0:T(8,128)} async-done(((f32[512,512]{1,0:T(8,128)}), f32[512,512]{1,0:T(8,128)}) %all-reduce.3.cloned.1.call-update) | async-done | bytes 1048592 | tf_op jit(solution)/shard_map/psum | solution.py:261
  322.6 0.0 copy-start.2
  322.6 1.2 copy-done.2
  323.8 53.4 %factorise.1 = (f32[512,512]{1,0:T(8,128)}, bf16[512,512]{1,0:T(8,128)(2,1)S(1)}, bf16[512,512]{1,0:T(8,128)(2,1)S(1)}) custom-call(f32[512,512]{1,0:T(8,128)S(1)} %copy-done.2, f32[512,512]{1,0:T(8,128)S(1)} %copy-done.1), custom_call_target="tpu_custom_call" | custom-call | flops 5368709120 | bytes 4194304 | tf_op jit(solution)/shard_map/factorise/pallas_call | solution.py:187
  377.2 0.0 all-to-all-done
  377.2 8.8 %last_product.1 = f32[8,256,512]{2,1,0:T(8,128)} custom-call(s32[8]{0:T(128)S(1)} %select_reduce_fusion.index_ref, f32[16,256,512]{2,1,0:T(8,128)} %bitcast.3.x_ref, bf16[512,512]{1,0:T(8,128)(2,1)S(1)} %get-tuple-element.5.mh_ref, bf16[512,512]{1,0:T(8,128)(2,1)S(1)} %get-tuple-element.6.ml_ref), custom_call_target="tpu_custom_call" | custom-call | tf_op jit(solution)/shard_map/last_product/pallas_call | solution.py:212
  (4 shorter events, 0.0 us)
Async XLA Ops:
  20.8 10.3 %copy-start.1 = (f32[512,512]{1,0:T(8,128)S(1)}, f32[512,512]{1,0:T(8,128)}, u32[]{:S(2)}) copy-start(f32[512,512]{1,0:T(8,128)} %r_ref.3) | copy-start | bytes 3145732
  20.8 356.4 %all-to-all-start = ((f32[4,4,256,512]{3,2,1,0:T(8,128)}), f32[4,4,256,512]{3,2,1,0:T(8,128)}, u32[]{:S(2)}, u32[]{:S(2)}) async-start(f32[4,4,256,512]{3,2,1,0:T(8,128)} %bitcast.6), calls=%async_computation | async-start | bytes 16777216 | tf_op jit(solution)/shard_map/all_to_all | solution.py:248
  31.1 291.5 %all-reduce.3.cloned.1.call-start = ((), (), s32[]{:S(2)}) async-start(), calls=%async_computation.1 | async-start | bytes 2097152 | tf_op jit(solution)/shard_map/psum | solution.py:261
  31.1 3.4 copy-start
  322.6 1.2 copy-start.2
Sparse Core Ops, SparseCore 0:
  37.6 284.9 all-reduce.2

commit v2 on v1

--- a/solution.py
+++ b/solution.py
@@ -10,6 +10,7 @@
 OWN_TILES = 8
 NB = 128
 HALF = 256
+FIRST = 48
 
 
 def split(x):
@@ -31,22 +32,27 @@
 
 
 def copy_kernel(index_ref, x_ref, o_ref):
-    o_ref[...] = x_ref[...]
-
-
-def gather_tiles(index, tiles):
-    block = (1,) + tiles.shape[1:]
+    o_ref[0] = x_ref[0, x_ref.shape[1] - o_ref.shape[1] :, :]
+
+
+def gather_rows(index, tiles, start, rows):
+    tile_rows, n = tiles.shape[1:]
+    taken = rows if start == 0 else tile_rows
     return pl.pallas_call(
         copy_kernel,
         grid_spec=pltpu.PrefetchScalarGridSpec(
             num_scalar_prefetch=1,
             grid=(index.shape[0],),
-            in_specs=[pl.BlockSpec(block, lambda i, idx: (idx[i], 0, 0))],
-            out_specs=pl.BlockSpec(block, lambda i, idx: (i, 0, 0)),
-        ),
-        out_shape=jax.ShapeDtypeStruct((index.shape[0],) + tiles.shape[1:], tiles.dtype),
-        name="gather_tiles",
+            in_specs=[pl.BlockSpec((1, taken, n), lambda i, idx: (idx[i], 0, 0))],
+            out_specs=pl.BlockSpec((1, rows, n), lambda i, idx: (i, 0, 0)),
+        ),
+        out_shape=jax.ShapeDtypeStruct((index.shape[0], rows, n), tiles.dtype),
+        name="gather_rows",
     )(index, tiles)
+
+
+def lower_blocks(n):
+    return [(i, j) for i in range(n // NB) for j in range(i + 1)]
 
 
 def gram_kernel(count_ref, x_ref, r_ref, g_ref, rh, rl, low, cross):
@@ -77,16 +83,17 @@
 
     @pl.when(i == pl.num_programs(0) - 1)
     def _():
-        c = cross[...]
-        g_ref[...] = c + c.T
-        g_ref[:HALF, :HALF] += low[:HALF, :HALF]
-        g_ref[HALF:, HALF:] += low[HALF:, HALF:]
-        corner = low[HALF:, :HALF]
-        g_ref[HALF:, :HALF] += corner
-        g_ref[:HALF, HALF:] += corner.T
-
-
-def local_gram(count, tiles, inverse_factor):
+        blocks = lower_blocks(low.shape[0])
+        for k, (bi, bj) in enumerate(blocks):
+            rows = slice(bi * NB, (bi + 1) * NB)
+            cols = slice(bj * NB, (bj + 1) * NB)
+            g_ref[k * NB : (k + 1) * NB, :] = low[rows, cols] + (cross[rows, cols] + cross[cols, rows].T)
+        used = len(blocks) * NB
+        if used < g_ref.shape[0]:
+            g_ref[used:, :] = jnp.zeros((g_ref.shape[0] - used, NB), jnp.float32)
+
+
+def local_gram(count, tiles, inverse_factor, packed):
     capacity, rows, n = tiles.shape
     return pl.pallas_call(
         gram_kernel,
@@ -99,7 +106,7 @@
                 ),
                 pl.BlockSpec((n, n), lambda i, c: (0, 0)),
             ],
-            out_specs=pl.BlockSpec((n, n), lambda i, c: (0, 0)),
+            out_specs=pl.BlockSpec((packed, NB), lambda i, c: (0, 0)),
             scratch_shapes=[
                 pltpu.VMEM((n, n), jnp.bfloat16),
                 pltpu.VMEM((n, n), jnp.bfloat16),
@@ -107,13 +114,107 @@
                 pltpu.VMEM((n, n), jnp.float32),
             ],
         ),
-        out_shape=jax.ShapeDtypeStruct((n, n), jnp.float32),
+        out_shape=jax.ShapeDtypeStruct((packed, NB), jnp.float32),
         compiler_params=pltpu.CompilerParams(vmem_limit_bytes=40 * 2**20),
         cost_estimate=pl.CostEstimate(
             flops=8 * capacity * rows * n * n, bytes_accessed=4 * capacity * rows * n, transcendentals=0
         ),
         name="local_gram",
     )(count, tiles, inverse_factor)
+
+
+def sum_kernel(scenes, rows, g_ref, note_ref, out_ref, notes_ref, h0, h1, rx0, rx1, rx2, ss, rs):
+    packed = g_ref.shape[0]
+    half, part, chunk = packed // 2, packed // rows, packed // rows // scenes
+    mates = rows // 2
+    scene = lax.axis_index("scene")
+    row = lax.axis_index("rows")
+    core = lax.rem(row, 2)
+    mate = lax.div(row, 2)
+    pair = (scene, row + 1 - 2 * core)
+    plane = [(scene, lax.rem(mate + d, mates) * 2 + core) for d in range(1, mates)]
+    line = [(lax.rem(scene + d, scenes), row) for d in range(1, scenes)]
+
+    barrier = pltpu.get_barrier_semaphore()
+    peers = [pair] + plane + line
+    for peer in peers:
+        pl.semaphore_signal(barrier, inc=1, device_id=peer, device_id_type=pl.DeviceIdType.MESH)
+    pl.semaphore_wait(barrier, len(peers))
+
+    used = [0]
+
+    def send(src, dst, peer):
+        k = used[0]
+        used[0] += 1
+        copy = pltpu.make_async_remote_copy(
+            src_ref=src, dst_ref=dst, send_sem=ss.at[k], recv_sem=rs.at[k],
+            device_id=peer, device_id_type=pl.DeviceIdType.MESH,
+        )
+        copy.start()
+        return copy
+
+    def span(start, size):
+        return pl.ds(pl.multiple_of(start, 8), size)
+
+    copy = send(g_ref.at[span((1 - core) * half, half)], rx0, pair)
+    copy.wait()
+    h0[...] = g_ref[span(core * half, half), :] + rx0[...]
+
+    copies = [send(h0.at[span(p[1] // 2 * part, part)], rx1.at[d], p) for d, p in enumerate(plane)]
+    total = h0[span(mate * part, part), :]
+    for d, copy in enumerate(copies):
+        copy.wait()
+        total += rx1[d]
+    h1[...] = total
+
+    copies = [send(h1.at[span(p[0] * chunk, chunk)], rx2.at[d], p) for d, p in enumerate(line)]
+    notes = [send(note_ref, notes_ref.at[scene], p) for p in line]
+    notes_ref[scene] = note_ref[...]
+    total = h1[span(scene * chunk, chunk), :]
+    for d, copy in enumerate(copies):
+        copy.wait()
+        total += rx2[d]
+
+    mine = core * half + mate * part
+    own = span(mine + scene * chunk, chunk)
+    out_ref[own, :] = total
+    for copy in [send(out_ref.at[own], out_ref.at[own], p) for p in line] + notes:
+        copy.wait()
+    own = span(mine, part)
+    for copy in [send(out_ref.at[own], out_ref.at[own], p) for p in plane]:
+        copy.wait()
+    own = span(core * half, half)
+    send(out_ref.at[own], out_ref.at[own], pair).wait()
+
+
+def sum_all(gram, note, scenes, rows):
+    packed = gram.shape[0]
+    half, part, chunk = packed // 2, packed // rows, packed // rows // scenes
+    copies = 2 + 2 * (rows // 2 - 1) + 3 * (scenes - 1)
+    whole = pl.BlockSpec(memory_space=pltpu.VMEM)
+    return pl.pallas_call(
+        functools.partial(sum_kernel, scenes, rows),
+        out_shape=[
+            jax.ShapeDtypeStruct(gram.shape, gram.dtype),
+            jax.ShapeDtypeStruct((scenes,) + note.shape, note.dtype),
+        ],
+        in_specs=[whole, whole],
+        out_specs=[whole, whole],
+        scratch_shapes=[
+            pltpu.VMEM((half, NB), jnp.float32),
+            pltpu.VMEM((part, NB), jnp.float32),
+            pltpu.VMEM((half, NB), jnp.float32),
+            pltpu.VMEM((rows // 2 - 1, part, NB), jnp.float32),
+            pltpu.VMEM((scenes - 1, chunk, NB), jnp.float32),
+            pltpu.SemaphoreType.DMA((copies,)),
+            pltpu.SemaphoreType.DMA((copies,)),
+        ],
+        compiler_params=pltpu.CompilerParams(
+            collective_id=0, has_side_effects=True, vmem_limit_bytes=24 * 2**20
+        ),
+        cost_estimate=pl.CostEstimate(flops=10 * packed * NB, bytes_accessed=16 * packed * NB, transcendentals=0),
+        name="sum_all",
+    )(gram, note)
 
 
 def eliminate(block):
@@ -146,8 +247,14 @@
 
 
 def factor_kernel(rows_all, g_ref, r_ref, u_ref, mh_ref, ml_ref, work):
-    n = g_ref.shape[0]
-    work[:, :n] = g_ref[...] / rows_all
+    n = r_ref.shape[0]
+    for b, (bi, bj) in enumerate(lower_blocks(n)):
+        rows = slice(bi * NB, (bi + 1) * NB)
+        cols = slice(bj * NB, (bj + 1) * NB)
+        block = g_ref[b * NB : (b + 1) * NB, :] / rows_all
+        work[rows, cols] = block
+        if bi != bj:
+            work[cols, rows] = block.T
     work[:, n:] = (
         lax.broadcasted_iota(jnp.int32, (n, n), 0) == lax.broadcasted_iota(jnp.int32, (n, n), 1)
     ).astype(jnp.float32)
@@ -183,7 +290,7 @@
 
 
 def factorise(gram, inverse_factor, rows_all):
-    n = gram.shape[0]
+    n = inverse_factor.shape[0]
     return pl.pallas_call(
         functools.partial(factor_kernel, rows_all),
         out_shape=[
@@ -200,27 +307,33 @@
     )(gram, inverse_factor)
 
 
-def last_kernel(index_ref, x_ref, mh_ref, ml_ref, o_ref):
-    a, b = upper_product(x_ref[0], mh_ref[...], ml_ref[...])
+def last_kernel(index_ref, first_ref, rest_ref, mh_ref, ml_ref, o_ref):
+    x = jnp.concatenate([first_ref[0], rest_ref[0]], axis=0)
+    a, b = upper_product(x, mh_ref[...], ml_ref[...])
     o_ref[0, :, :HALF] = a
     o_ref[0, :, HALF:] = b
 
 
-def last_product(index, tiles, mh, ml):
-    rows, n = tiles.shape[1:]
+def last_product(index, first, rest, mh, ml):
+    n = first.shape[2]
+    rows = first.shape[1] + rest.shape[1]
     whole = pl.BlockSpec((n, n), lambda i, idx: (0, 0))
+
+    def tiles(x):
+        return pl.BlockSpec((1,) + x.shape[1:], lambda i, idx: (idx[i], 0, 0))
+
     return pl.pallas_call(
         last_kernel,
         grid_spec=pltpu.PrefetchScalarGridSpec(
             num_scalar_prefetch=1,
             grid=(OWN_TILES,),
-            in_specs=[pl.BlockSpec((1, rows, n), lambda i, idx: (idx[i], 0, 0)), whole, whole],
+            in_specs=[tiles(first), tiles(rest), whole, whole],
             out_specs=pl.BlockSpec((1, rows, n), lambda i, idx: (i, 0, 0)),
         ),
         out_shape=jax.ShapeDtypeStruct((OWN_TILES, rows, n), jnp.float32),
         compiler_params=pltpu.CompilerParams(vmem_limit_bytes=32 * 2**20),
         name="last_product",
-    )(index, tiles, mh, ml)
+    )(index, first, rest, mh, ml)
 
 
 def seats(owner, count, scenes):
@@ -244,23 +357,34 @@
     target = jnp.where(is_live, tile_owner * pair_most + rank, -1)
     selector = (target[None, :] == position[:, None]).astype(jnp.int32)
     chosen = (selector * position[None, :]).sum(1)
-    outgoing = gather_tiles(chosen, observations)
-    received = lax.all_to_all(
-        outgoing.reshape(scenes, pair_most, tile_rows, n), "scene", split_axis=0, concat_axis=0, tiled=True
-    ).reshape(capacity, tile_rows, n)
+
+    def exchange(outgoing):
+        rows = outgoing.shape[1]
+        return lax.all_to_all(
+            outgoing.reshape(scenes, pair_most, rows, n), "scene", split_axis=0, concat_axis=0, tiled=True
+        ).reshape(capacity, rows, n)
+
+    first, count = lax.optimization_barrier((gather_rows(chosen, observations, 0, FIRST), tile_count))
+    first = exchange(first)
+    rest = gather_rows(chosen, observations, FIRST, tile_rows - FIRST)
 
     me = lax.axis_index("scene")
     note = jnp.where(is_live, (tile_owner * pair_most + rank) * OWN_TILES + tile_slot, -1)
-    notes = lax.all_gather(note, "scene")
+    note = jnp.zeros((8, 128), jnp.int32).at[0, :capacity].set(note)
+    chunk = -(-len(lower_blocks(n)) * NB // devices // 8) * 8
+    gram = local_gram(count, observations, inverse_factor, chunk * devices)
+    gram, notes = sum_all(gram, note, scenes, lax.axis_size("rows"))
+    rest, gram = lax.optimization_barrier((rest, gram))
+    rest = exchange(rest)
+    notes = notes[:, 0, :capacity]
     seat = notes // OWN_TILES
     mine = (notes >= 0) & (seat // pair_most == me)
     place = jnp.arange(scenes, dtype=jnp.int32)[:, None] * pair_most + seat % pair_most
     match = mine[None] & ((notes % OWN_TILES)[None] == jnp.arange(OWN_TILES, dtype=jnp.int32)[:, None, None])
     order = jnp.where(match, place[None], 0).sum((1, 2))
 
-    gram = lax.psum(local_gram(tile_count, observations, inverse_factor), ("scene", "rows"))
     factor, mh, ml = factorise(gram, inverse_factor, devices * OWN_TILES * tile_rows)
-    return last_product(order, received, mh, ml), factor
+    return last_product(order, first, rest, mh, ml), factor
 
 
 def solution(mesh):

time: 394 us -> 244 us (0.62)
  blocking collectives: 183 us -> 0 us
  Pallas kernels: 73 us -> 130 us
  between operations: 15.4 us -> 1.36 us
  waiting for transfers between devices: 102 us -> 95.2 us
    unnamed x1 -> x0, blocking collectives: 183 us -> none
    psum x1 -> x0, waiting for transfers between devices: 102 us -> none  [shards(): lax.psum(local_gram(tile_count, observations, inverse_factor), ('scene',...]
    all_to_all x1 -> x2, waiting for transfers between devices: 0.01 us -> 95.2 us  [exchange(): lax.all_to_all(outgoing.reshape(scenes, pair_most, rows, n), 'scene', spl...]
    pallas_call x1 -> x3, Pallas kernels: 8.71 us -> 50.1 us  [the longest x1 27.7 us: sum_all(): pl.pallas_call(functools.partial(sum_kernel, scenes, rows), out_shape=[ja...]
    pallas_call x1, Pallas kernels: 2.13 us -> 17.5 us  [local_gram(): pl.pallas_call(gram_kernel, grid_spec=pltpu.PrefetchScalarGridSpec(num_sc...]
    all_to_all x1 -> x2, starting transfers between devices: 10.3 us -> 9.47 us  [exchange(): lax.all_to_all(outgoing.reshape(scenes, pair_most, rows, n), 'scene', spl...]
  transfers between devices with their start and end apart: 2 -> 2, of which waited for: 1 -> 1; matrix products, arithmetic and copies ran while one was open for 0% -> 0% of each run, Pallas kernels for 14% -> 46%
where the time goes in v2:
time: 244 us; the launch traced here: 243 us
  Pallas kernels  130 us (53%)
  waiting for transfers between devices  95.2 us (39%)
  starting transfers between devices  9.47 us (4%)
  local copies, waits for them, and re-layouts  4.61 us (2%)
  other arithmetic  2.46 us (1%)
    all_to_all x2, waiting for transfers between devices, exchange(): lax.all_to_all(outgoing.reshape(scenes, pair_most, rows, n), 'scene', spl...  95.2 us
    pallas_call x1, Pallas kernels, factorise(): pl.pallas_call(functools.partial(factor_kernel, rows_all), out_shape=[jax...  53.5 us
    pallas_call x1, Pallas kernels, sum_all(): pl.pallas_call(functools.partial(sum_kernel, scenes, rows), out_shape=[ja...  27.7 us
    pallas_call x2, Pallas kernels, gather_rows(): pl.pallas_call(copy_kernel, grid_spec=pltpu.PrefetchScalarGridSpec(num_sc...  22.3 us
    pallas_call x1, Pallas kernels, local_gram(): pl.pallas_call(gram_kernel, grid_spec=pltpu.PrefetchScalarGridSpec(num_sc...  17.5 us
    all_to_all x2, starting transfers between devices, exchange(): lax.all_to_all(outgoing.reshape(scenes, pair_most, rows, n), 'scene', spl...  9.47 us
    pallas_call x1, Pallas kernels, last_product(): pl.pallas_call(last_kernel, grid_spec=pltpu.PrefetchScalarGridSpec(num_sc...  8.63 us
  transfers between devices with their start and end apart: 2, of which 1 were waited for; matrix products, arithmetic and copies ran while one was open for 0% of the time, Pallas kernels for 46%

profile of v2, /device:TPU:0, one launch (start us, length us, event | category | flops | bytes accessed | tf_op | source)
XLA Modules:
  0.0 242.8 jit_solution(16159263115630858180)
XLA Ops:
  1.3 0.9 convert_reduce_fusion
  2.2 0.7 select_bitcast_fusion
  2.9 0.6 select_reduce_fusion.1.index_ref
  3.5 10.0 %gather_rows.2 = f32[16,48,512]{2,1,0:T(8,128)} custom-call(s32[16]{0:T(128)} %select_reduce_fusion.1.index_ref, f32[16,256,512]{2,1,0:T(8,128)} %x_ref.5), custom_call_target="tpu_custom_call" | custom-call | tf_op jit(solution)/shard_map/gather_rows/pallas_call | solution.py:41
  13.5 4.1 %all-to-all-start = ((f32[4,4,48,512]{3,2,1,0:T(8,128)}), f32[4,4,48,512]{3,2,1,0:T(8,128)S(1)}, u32[]{:S(2)}, u32[]{:S(2)}) async-start(f32[4,4,48,512]{3,2,1,0:T(8,128)} %bitcast.12), calls=%async_computation | async-start | bytes 3145728 | tf_op jit(solution)/shard_map/all_to_all | solution.py:363
  17.6 0.0 copy-start.1
  17.6 12.3 %gather_rows.3 = f32[16,208,512]{2,1,0:T(8,128)} custom-call(s32[16]{0:T(128)} %select_reduce_fusion.1.index_ref, f32[16,256,512]{2,1,0:T(8,128)} %x_ref.5), custom_call_target="tpu_custom_call" | custom-call | tf_op jit(solution)/shard_map/gather_rows/pallas_call | solution.py:41
  29.9 0.0 copy-done.1
  30.0 0.0 copy-start
  30.0 3.4 %copy-done = f32[16,256,512]{2,1,0:T(8,128)S(1)} copy-done((f32[16,256,512]{2,1,0:T(8,128)S(1)}, f32[16,256,512]{2,1,0:T(8,128)}, u32[]{:S(2)}) %copy-start) | copy-done | bytes 8388632
  33.3 17.5 %local_gram.1.g_ref = f32[1280,128]{1,0:T(8,128)S(1)} custom-call(s32[1]{0:T(128)} %copy.7.count_ref, f32[16,256,512]{2,1,0:T(8,128)S(1)} %copy-done, f32[512,512]{1,0:T(8,128)S(1)} %copy-done.1), custom_call_target="tpu_custom_call" | custom-call | flops 8589934592 | bytes 8388608 | tf_op jit(solution)/shard_map/local_gram/pallas_call | solution.py:98
  50.9 27.7 %sum_all.1 = (f32[1280,128]{1,0:T(8,128)S(1)}, s32[4,8,128]{2,1,0:T(8,128)S(1)}) custom-call(f32[1280,128]{1,0:T(8,128)S(1)} %local_gram.1.g_ref, s32[8,128]{1,0:T(8,128)S(1)} %scatter.4.note_ref), custom_call_target="tpu_custom_call" | custom-call | flops 1638400 | bytes 2621440 | tf_op jit(solution)/shard_map/sum_all/pallas_call | solution.py:195
  78.6 0.0 all-to-all-done
  78.6 5.4 %all-to-all-start.1 = ((f32[4,4,208,512]{3,2,1,0:T(8,128)}), f32[4,4,208,512]{3,2,1,0:T(8,128)}, u32[]{:S(2)}, u32[]{:S(2)}) async-start(f32[4,4,208,512]{3,2,1,0:T(8,128)} %bitcast.11), calls=%async_computation.1 | async-start | bytes 13631488 | tf_op jit(solution)/shard_map/all_to_all | solution.py:363
  84.1 0.1 add_select_fusion.1
  84.1 0.1 select_reduce_fusion.index_ref
  84.3 0.0 copy-start.2
  84.3 1.2 copy-done.2
  85.5 53.5 %factorise.1 = (f32[512,512]{1,0:T(8,128)}, bf16[512,512]{1,0:T(8,128)(2,1)S(1)}, bf16[512,512]{1,0:T(8,128)(2,1)S(1)}) custom-call(f32[1280,128]{1,0:T(8,128)S(1)} %get-tuple-element.28.g_ref, f32[512,512]{1,0:T(8,128)S(1)} %copy-done.2), custom_call_target="tpu_custom_call" | custom-call | flops 5368709120 | bytes 4194304 | tf_op jit(solution)/shard_map/factorise/pallas_call | solution.py:294
  139.0 95.2 %all-to-all-done.1 = f32[4,4,208,512]{3,2,1,0:T(8,128)} async-done(((f32[4,4,208,512]{3,2,1,0:T(8,128)}), f32[4,4,208,512]{3,2,1,0:T(8,128)}, u32[]{:S(2)}, u32[]{:S(2)}) %all-to-all-start.1) | async-done | bytes 6815776 | tf_op jit(solution)/shard_map/all_to_all | solution.py:363
  234.2 8.6 %last_product.1 = f32[8,256,512]{2,1,0:T(8,128)} custom-call(s32[8]{0:T(128)S(1)} %select_reduce_fusion.index_ref, f32[16,48,512]{2,1,0:T(8,128)S(1)} %bitcast.10, f32[16,208,512]{2,1,0:T(8,128)} %bitcast.6.rest_ref, bf16[512,512]{1,0:T(8,128)(2,1)S(1)} %get-tuple-element.29.mh_ref, bf16[512,512]{1,0:T(8,128)(2,1)S(1)} %get-tuple-element.30.ml_ref), custom_call_target="tpu_custom_call" | custom-call | tf_op jit(solution)/shard_map/last_product/pallas_call | solution.py:325
  (5 shorter events, 0.0 us)
Async XLA Ops:
  13.5 65.2 %all-to-all-start = ((f32[4,4,48,512]{3,2,1,0:T(8,128)}), f32[4,4,48,512]{3,2,1,0:T(8,128)S(1)}, u32[]{:S(2)}, u32[]{:S(2)}) async-start(f32[4,4,48,512]{3,2,1,0:T(8,128)} %bitcast.12), calls=%async_computation | async-start | bytes 3145728 | tf_op jit(solution)/shard_map/all_to_all | solution.py:363
  17.6 12.4 %copy-start.1 = (f32[512,512]{1,0:T(8,128)S(1)}, f32[512,512]{1,0:T(8,128)}, u32[]{:S(2)}) copy-start(f32[512,512]{1,0:T(8,128)} %r_ref.3) | copy-start | bytes 3145732
  30.0 3.4 %copy-start = (f32[16,256,512]{2,1,0:T(8,128)S(1)}, f32[16,256,512]{2,1,0:T(8,128)}, u32[]{:S(2)}) copy-start(f32[16,256,512]{2,1,0:T(8,128)} %x_ref.5) | copy-start | bytes 25165828
  78.6 155.6 %all-to-all-start.1 = ((f32[4,4,208,512]{3,2,1,0:T(8,128)}), f32[4,4,208,512]{3,2,1,0:T(8,128)}, u32[]{:S(2)}, u32[]{:S(2)}) async-start(f32[4,4,208,512]{3,2,1,0:T(8,128)} %bitcast.11), calls=%async_computation.1 | async-start | bytes 13631488 | tf_op jit(solution)/shard_map/all_to_all | solution.py:363
  84.3 1.2 copy-start.2

commit v3 on v2

--- a/solution.py
+++ b/solution.py
@@ -10,7 +10,9 @@
 OWN_TILES = 8
 NB = 128
 HALF = 256
-FIRST = 48
+FIRST = 64
+LAST = 64
+PER_STEP = 4
 
 
 def split(x):
@@ -31,22 +33,28 @@
     return a, b
 
 
-def copy_kernel(index_ref, x_ref, o_ref):
-    o_ref[0] = x_ref[0, x_ref.shape[1] - o_ref.shape[1] :, :]
-
-
-def gather_rows(index, tiles, start, rows):
-    tile_rows, n = tiles.shape[1:]
-    taken = rows if start == 0 else tile_rows
-    return pl.pallas_call(
-        copy_kernel,
-        grid_spec=pltpu.PrefetchScalarGridSpec(
-            num_scalar_prefetch=1,
-            grid=(index.shape[0],),
-            in_specs=[pl.BlockSpec((1, taken, n), lambda i, idx: (idx[i], 0, 0))],
-            out_specs=pl.BlockSpec((1, rows, n), lambda i, idx: (i, 0, 0)),
-        ),
-        out_shape=jax.ShapeDtypeStruct((index.shape[0], rows, n), tiles.dtype),
+def copy_kernel(starts, index_ref, x_ref, *refs):
+    outs, sems = refs[:-1], refs[-1]
+    copies = []
+    for p, (start, o_ref) in enumerate(zip(starts, outs)):
+        for i in range(o_ref.shape[0]):
+            source = x_ref.at[index_ref[i], pl.ds(start, o_ref.shape[1]), :]
+            copies.append(pltpu.make_async_copy(source, o_ref.at[i], sems.at[p, i]))
+    for copy in copies:
+        copy.start()
+    for copy in copies:
+        copy.wait()
+
+
+def gather_rows(index, tiles, spans):
+    count = index.shape[0]
+    anywhere = pl.BlockSpec(memory_space=pl.ANY)
+    return pl.pallas_call(
+        functools.partial(copy_kernel, [start for start, _ in spans]),
+        in_specs=[pl.BlockSpec(memory_space=pltpu.SMEM), anywhere],
+        out_specs=[anywhere] * len(spans),
+        out_shape=[jax.ShapeDtypeStruct((count, rows, tiles.shape[2]), tiles.dtype) for _, rows in spans],
+        scratch_shapes=[pltpu.SemaphoreType.DMA((len(spans), count))],
         name="gather_rows",
     )(index, tiles)
 
@@ -123,24 +131,19 @@
     )(count, tiles, inverse_factor)
 
 
-def sum_kernel(scenes, rows, g_ref, note_ref, out_ref, notes_ref, h0, h1, rx0, rx1, rx2, ss, rs):
-    packed = g_ref.shape[0]
-    half, part, chunk = packed // 2, packed // rows, packed // rows // scenes
-    mates = rows // 2
-    scene = lax.axis_index("scene")
+def place():
     row = lax.axis_index("rows")
-    core = lax.rem(row, 2)
-    mate = lax.div(row, 2)
-    pair = (scene, row + 1 - 2 * core)
-    plane = [(scene, lax.rem(mate + d, mates) * 2 + core) for d in range(1, mates)]
-    line = [(lax.rem(scene + d, scenes), row) for d in range(1, scenes)]
-
+    return lax.axis_index("scene"), row, lax.rem(row, 2), lax.div(row, 2)
+
+
+def greet(peers):
     barrier = pltpu.get_barrier_semaphore()
-    peers = [pair] + plane + line
     for peer in peers:
         pl.semaphore_signal(barrier, inc=1, device_id=peer, device_id_type=pl.DeviceIdType.MESH)
     pl.semaphore_wait(barrier, len(peers))
 
+
+def sender(ss, rs):
     used = [0]
 
     def send(src, dst, peer):
@@ -153,14 +156,29 @@
         copy.start()
         return copy
 
-    def span(start, size):
-        return pl.ds(pl.multiple_of(start, 8), size)
+    return send
+
+
+def span(start, size):
+    return pl.ds(pl.multiple_of(start, 8), size)
+
+
+def sum_kernel(scenes, rows, g_ref, note_ref, out_ref, notes_ref, h0, h1, rx0, rx1, rx2, ss, rs):
+    packed = g_ref.shape[0]
+    half, part, chunk = packed // 2, packed // rows, packed // rows // scenes
+    mates = rows // 2
+    scene, row, core, mate = place()
+    pair = (scene, row + 1 - 2 * core)
+    plane = [(scene, lax.rem(mate + d, mates) * 2 + core) for d in range(1, mates)]
+    line = [(lax.rem(scene + d, scenes), row) for d in range(1, scenes)]
+    greet([pair] + plane + line)
+    send = sender(ss, rs)
 
     copy = send(g_ref.at[span((1 - core) * half, half)], rx0, pair)
     copy.wait()
     h0[...] = g_ref[span(core * half, half), :] + rx0[...]
 
-    copies = [send(h0.at[span(p[1] // 2 * part, part)], rx1.at[d], p) for d, p in enumerate(plane)]
+    copies = [send(h0.at[span(lax.div(p[1], 2) * part, part)], rx1.at[d], p) for d, p in enumerate(plane)]
     total = h0[span(mate * part, part), :]
     for d, copy in enumerate(copies):
         copy.wait()
@@ -175,27 +193,21 @@
         copy.wait()
         total += rx2[d]
 
-    mine = core * half + mate * part
-    own = span(mine + scene * chunk, chunk)
+    own = span(scene * chunk, chunk)
     out_ref[own, :] = total
     for copy in [send(out_ref.at[own], out_ref.at[own], p) for p in line] + notes:
         copy.wait()
-    own = span(mine, part)
-    for copy in [send(out_ref.at[own], out_ref.at[own], p) for p in plane]:
-        copy.wait()
-    own = span(core * half, half)
-    send(out_ref.at[own], out_ref.at[own], pair).wait()
-
-
-def sum_all(gram, note, scenes, rows):
+
+
+def sum_part(gram, note, scenes, rows):
     packed = gram.shape[0]
     half, part, chunk = packed // 2, packed // rows, packed // rows // scenes
-    copies = 2 + 2 * (rows // 2 - 1) + 3 * (scenes - 1)
+    copies = rows // 2 + 3 * (scenes - 1)
     whole = pl.BlockSpec(memory_space=pltpu.VMEM)
     return pl.pallas_call(
         functools.partial(sum_kernel, scenes, rows),
         out_shape=[
-            jax.ShapeDtypeStruct(gram.shape, gram.dtype),
+            jax.ShapeDtypeStruct((part, NB), gram.dtype),
             jax.ShapeDtypeStruct((scenes,) + note.shape, note.dtype),
         ],
         in_specs=[whole, whole],
@@ -213,8 +225,43 @@
             collective_id=0, has_side_effects=True, vmem_limit_bytes=24 * 2**20
         ),
         cost_estimate=pl.CostEstimate(flops=10 * packed * NB, bytes_accessed=16 * packed * NB, transcendentals=0),
-        name="sum_all",
+        name="sum_part",
     )(gram, note)
+
+
+def spread_kernel(rows, h_ref, out_ref, ss, rs):
+    packed = out_ref.shape[0]
+    half, part = packed // 2, packed // rows
+    mates = rows // 2
+    scene, row, core, mate = place()
+    pair = (scene, row + 1 - 2 * core)
+    plane = [(scene, lax.rem(mate + d, mates) * 2 + core) for d in range(1, mates)]
+    greet([pair] + plane)
+    send = sender(ss, rs)
+    own = span(core * half + mate * part, part)
+    copies = [send(h_ref, out_ref.at[own], p) for p in plane]
+    out_ref[own, :] = h_ref[...]
+    for copy in copies:
+        copy.wait()
+    own = span(core * half, half)
+    send(out_ref.at[own], out_ref.at[own], pair).wait()
+
+
+def spread(part_sum, rows):
+    whole = pl.BlockSpec(memory_space=pltpu.VMEM)
+    packed = part_sum.shape[0] * rows
+    return pl.pallas_call(
+        functools.partial(spread_kernel, rows),
+        out_shape=jax.ShapeDtypeStruct((packed, NB), part_sum.dtype),
+        in_specs=[whole],
+        out_specs=whole,
+        scratch_shapes=[pltpu.SemaphoreType.DMA((rows // 2,)), pltpu.SemaphoreType.DMA((rows // 2,))],
+        compiler_params=pltpu.CompilerParams(
+            collective_id=1, has_side_effects=True, vmem_limit_bytes=24 * 2**20
+        ),
+        cost_estimate=pl.CostEstimate(flops=packed * NB, bytes_accessed=8 * packed * NB, transcendentals=0),
+        name="spread",
+    )(part_sum)
 
 
 def eliminate(block):
@@ -307,33 +354,47 @@
     )(gram, inverse_factor)
 
 
-def last_kernel(index_ref, first_ref, rest_ref, mh_ref, ml_ref, o_ref):
-    x = jnp.concatenate([first_ref[0], rest_ref[0]], axis=0)
+def last_kernel(pieces, index_ref, *refs):
+    mh_ref, ml_ref = refs[PER_STEP * pieces : PER_STEP * pieces + 2]
+    o_ref = refs[-1]
+    x = jnp.concatenate([r[0] for r in refs[: PER_STEP * pieces]], axis=0)
     a, b = upper_product(x, mh_ref[...], ml_ref[...])
-    o_ref[0, :, :HALF] = a
-    o_ref[0, :, HALF:] = b
-
-
-def last_product(index, first, rest, mh, ml):
-    n = first.shape[2]
-    rows = first.shape[1] + rest.shape[1]
+    shape = (PER_STEP, o_ref.shape[1], HALF)
+    o_ref[:, :, :HALF] = a.reshape(shape)
+    o_ref[:, :, HALF:] = b.reshape(shape)
+
+
+def last_product(index, pieces, mh, ml, tile_rows, block, before=None):
+    n = mh.shape[0]
+    rows = sum(x.shape[1] for x in pieces)
     whole = pl.BlockSpec((n, n), lambda i, idx: (0, 0))
 
-    def tiles(x):
-        return pl.BlockSpec((1,) + x.shape[1:], lambda i, idx: (idx[i], 0, 0))
-
-    return pl.pallas_call(
-        last_kernel,
+    def tile(x, t):
+        return pl.BlockSpec((1,) + x.shape[1:], lambda i, idx: (idx[i * PER_STEP + t], 0, 0))
+
+    operands = [x for _ in range(PER_STEP) for x in pieces] + [mh, ml]
+    specs = [tile(x, t) for t in range(PER_STEP) for x in pieces] + [whole, whole]
+    aliases = {}
+    if before is not None:
+        aliases = {1 + len(operands): 0}
+        operands.append(before)
+        specs.append(pl.BlockSpec(memory_space=pl.ANY))
+    return pl.pallas_call(
+        functools.partial(last_kernel, len(pieces)),
         grid_spec=pltpu.PrefetchScalarGridSpec(
             num_scalar_prefetch=1,
-            grid=(OWN_TILES,),
-            in_specs=[tiles(first), tiles(rest), whole, whole],
-            out_specs=pl.BlockSpec((1, rows, n), lambda i, idx: (i, 0, 0)),
-        ),
-        out_shape=jax.ShapeDtypeStruct((OWN_TILES, rows, n), jnp.float32),
-        compiler_params=pltpu.CompilerParams(vmem_limit_bytes=32 * 2**20),
+            grid=(OWN_TILES // PER_STEP,),
+            in_specs=specs,
+            out_specs=pl.BlockSpec((PER_STEP, rows, n), lambda i, idx: (i, block, 0)),
+        ),
+        out_shape=jax.ShapeDtypeStruct((OWN_TILES, tile_rows, n), jnp.float32),
+        input_output_aliases=aliases,
+        compiler_params=pltpu.CompilerParams(vmem_limit_bytes=40 * 2**20),
+        cost_estimate=pl.CostEstimate(
+            flops=6 * OWN_TILES * rows * n * n, bytes_accessed=8 * OWN_TILES * rows * n, transcendentals=0
+        ),
         name="last_product",
-    )(index, first, rest, mh, ml)
+    )(index, *operands)
 
 
 def seats(owner, count, scenes):
@@ -364,18 +425,23 @@
             outgoing.reshape(scenes, pair_most, rows, n), "scene", split_axis=0, concat_axis=0, tiled=True
         ).reshape(capacity, rows, n)
 
-    first, count = lax.optimization_barrier((gather_rows(chosen, observations, 0, FIRST), tile_count))
+    first, count = lax.optimization_barrier((gather_rows(chosen, observations, [(0, FIRST)])[0], tile_count))
     first = exchange(first)
-    rest = gather_rows(chosen, observations, FIRST, tile_rows - FIRST)
+    middle, rest = gather_rows(
+        chosen, observations, [(FIRST, tile_rows - FIRST - LAST), (tile_rows - LAST, LAST)]
+    )
 
     me = lax.axis_index("scene")
     note = jnp.where(is_live, (tile_owner * pair_most + rank) * OWN_TILES + tile_slot, -1)
     note = jnp.zeros((8, 128), jnp.int32).at[0, :capacity].set(note)
     chunk = -(-len(lower_blocks(n)) * NB // devices // 8) * 8
     gram = local_gram(count, observations, inverse_factor, chunk * devices)
-    gram, notes = sum_all(gram, note, scenes, lax.axis_size("rows"))
-    rest, gram = lax.optimization_barrier((rest, gram))
+    rows = lax.axis_size("rows")
+    part_sum, notes = sum_part(gram, note, scenes, rows)
+    middle, rest, part_sum = lax.optimization_barrier((middle, rest, part_sum))
+    middle = exchange(middle)
     rest = exchange(rest)
+    gram = spread(part_sum, rows)
     notes = notes[:, 0, :capacity]
     seat = notes // OWN_TILES
     mine = (notes >= 0) & (seat // pair_most == me)
@@ -384,7 +450,8 @@
     order = jnp.where(match, place[None], 0).sum((1, 2))
 
     factor, mh, ml = factorise(gram, inverse_factor, devices * OWN_TILES * tile_rows)
-    return last_product(order, first, rest, mh, ml), factor
+    most = last_product(order, [first, middle], mh, ml, tile_rows, 0)
+    return last_product(order, [rest], mh, ml, tile_rows, tile_rows // LAST - 1, most), factor
 
 
 def solution(mesh):

time: 244 us -> 483 us (1.98)
  Pallas kernels: 130 us -> 364 us
  blocking collectives: 0 us -> 97.5 us
  waiting for transfers between devices: 95.2 us -> 0.01 us
    pallas_call x4 -> x6, Pallas kernels: 58.7 us -> 303 us  [the longest x2 258 us: gather_rows(): pl.pallas_call(functools.partial(copy_kernel, [start for start, _ in span...]
    all_to_all x0 -> x1, blocking collectives: none -> 97.5 us  [exchange(): lax.all_to_all(outgoing.reshape(scenes, pair_most, rows, n), 'scene', spl...]
    all_to_all x2, waiting for transfers between devices: 95.2 us -> 0.01 us  [exchange(): lax.all_to_all(outgoing.reshape(scenes, pair_most, rows, n), 'scene', spl...]
    pallas_call x1, Pallas kernels: 17.5 us -> 7.14 us  [local_gram(): pl.pallas_call(gram_kernel, grid_spec=pltpu.PrefetchScalarGridSpec(num_sc...]
  transfers between devices with their start and end apart: 2 -> 2, of which waited for: 1 -> 0; matrix products, arithmetic and copies ran while one was open for 0% -> 0% of each run, Pallas kernels for 46% -> 61%
where the time goes in v3:
time: 483 us; the launch traced here: 482 us
  Pallas kernels  364 us (75%)
  blocking collectives  97.5 us (20%)
  starting transfers between devices  10.8 us (2%)
  local copies, waits for them, and re-layouts  6.53 us (1%)
    pallas_call x2, Pallas kernels, gather_rows(): pl.pallas_call(functools.partial(copy_kernel, [start for start, _ in span...  258 us
    all_to_all x1, blocking collectives, exchange(): lax.all_to_all(outgoing.reshape(scenes, pair_most, rows, n), 'scene', spl...  97.5 us
    pallas_call x1, Pallas kernels, factorise(): pl.pallas_call(functools.partial(factor_kernel, rows_all), out_shape=[jax...  53.5 us
    pallas_call x1, Pallas kernels, sum_part(): pl.pallas_call(functools.partial(sum_kernel, scenes, rows), out_shape=[ja...  29.8 us
    all_to_all x2, starting transfers between devices, exchange(): lax.all_to_all(outgoing.reshape(scenes, pair_most, rows, n), 'scene', spl...  10.8 us
  transfers between devices with their start and end apart: 2, of which 0 were waited for; matrix products, arithmetic and copies ran while one was open for 0% of the time, Pallas kernels for 61%

profile of v3, /device:TPU:0, one launch (start us, length us, event | category | flops | bytes accessed | tf_op | source)
XLA Modules:
  0.0 482.5 jit_solution(2357991867942043447)
XLA Ops:
  1.3 0.9 convert_reduce_fusion
  2.2 0.7 select_bitcast_fusion
  2.9 0.7 select_reduce_fusion.1.index_ref
  3.6 65.4 %gather_rows.2 = f32[16,64,512]{2,1,0:T(8,128)} custom-call(s32[16]{0:T(128)} %select_reduce_fusion.1.index_ref, f32[16,256,512]{2,1,0:T(8,128)} %x_ref.5), custom_call_target="tpu_custom_call" | custom-call | tf_op jit(solution)/shard_map/gather_rows/pallas_call | solution.py:52
  69.0 6.3 %all-to-all-start.1 = ((f32[4,4,64,512]{3,2,1,0:T(8,128)}), f32[4,4,64,512]{3,2,1,0:T(8,128)S(1)}, u32[]{:S(2)}, u32[]{:S(2)}) async-start(f32[4,4,64,512]{3,2,1,0:T(8,128)} %bitcast.20), calls=%async_computation.1 | async-start | bytes 4194304 | tf_op jit(solution)/shard_map/all_to_all | solution.py:424
  75.4 0.0 copy-start.4
  75.4 192.8 %gather_rows.3 = (f32[16,128,512]{2,1,0:T(8,128)}, f32[16,64,512]{2,1,0:T(8,128)}) custom-call(s32[16]{0:T(128)} %select_reduce_fusion.1.index_ref, f32[16,256,512]{2,1,0:T(8,128)} %x_ref.5), custom_call_target="tpu_custom_call" | custom-call | tf_op jit(solution)/shard_map/gather_rows/pallas_call | solution.py:52
  268.2 0.0 copy-done.4
  268.2 0.0 copy-start.1
  268.2 3.4 copy-done.1
  271.5 7.1 %local_gram.1.g_ref = f32[1280,128]{1,0:T(8,128)S(1)} custom-call(s32[1]{0:T(128)} %copy.9.count_ref, f32[16,256,512]{2,1,0:T(8,128)S(1)} %copy-done.1, f32[512,512]{1,0:T(8,128)S(1)} %copy-done.4), custom_call_target="tpu_custom_call" | custom-call | flops 8589934592 | bytes 8388608 | tf_op jit(solution)/shard_map/local_gram/pallas_call | solution.py:106
  278.7 29.8 %sum_part.1 = (f32[160,128]{1,0:T(8,128)S(1)}, s32[4,8,128]{2,1,0:T(8,128)S(1)}) custom-call(f32[1280,128]{1,0:T(8,128)S(1)} %local_gram.1.g_ref, s32[8,128]{1,0:T(8,128)S(1)} %scatter.4.note_ref), custom_call_target="tpu_custom_call" | custom-call | flops 1638400 | bytes 2621440 | tf_op jit(solution)/shard_map/sum_part/pallas_call | solution.py:207
  308.5 0.0 all-to-all-done.1
  308.6 97.5 %all_to_all.15 = f32[4,4,128,512]{3,2,1,0:T(8,128)} all-to-all(f32[4,4,128,512]{3,2,1,0:T(8,128)} %bitcast.21), channel_id=1, replica_groups=mesh['scene'=4,'rows'=8] {'scene'}, dimensions={0} | all-to-all | bytes 8388608 | tf_op jit(solution)/shard_map/all_to_all | solution.py:424
  406.0 4.5 all-to-all-start
  410.5 7.6 %spread.1.g_ref = f32[1280,128]{1,0:T(8,128)S(1)} custom-call(f32[160,128]{1,0:T(8,128)S(1)} %get-tuple-element.32.h_ref), custom_call_target="tpu_custom_call" | custom-call | flops 163840 | bytes 1310720 | tf_op jit(solution)/shard_map/spread/pallas_call | solution.py:253
  418.2 0.0 copy-start.2
  418.2 0.8 copy-done.2
  419.0 0.1 add_select_fusion.1
  419.1 0.1 select_reduce_fusion.index_ref
  419.2 0.0 copy-start.3
  419.2 1.1 copy-done.3
  420.3 0.0 copy-start.5
  420.3 1.2 copy-done.5
  421.5 0.0 copy-start
  421.5 53.5 %factorise.1 = (f32[512,512]{1,0:T(8,128)}, bf16[512,512]{1,0:T(8,128)(2,1)S(1)}, bf16[512,512]{1,0:T(8,128)(2,1)S(1)}) custom-call(f32[1280,128]{1,0:T(8,128)S(1)} %copy-done.3, f32[512,512]{1,0:T(8,128)S(1)} %copy-done.5), custom_call_target="tpu_custom_call" | custom-call | flops 5368709120 | bytes 4194304 | tf_op jit(solution)/shard_map/factorise/pallas_call | solution.py:341
  475.0 0.0 copy-done
  475.0 3.9 last_product.2.refs_6_
  479.0 0.0 all-to-all-done
  479.0 3.5 last_product.3
  (5 shorter events, 0.0 us)
Async XLA Ops:
  69.0 239.5 %all-to-all-start.1 = ((f32[4,4,64,512]{3,2,1,0:T(8,128)}), f32[4,4,64,512]{3,2,1,0:T(8,128)S(1)}, u32[]{:S(2)}, u32[]{:S(2)}) async-start(f32[4,4,64,512]{3,2,1,0:T(8,128)} %bitcast.20), calls=%async_computation.1 | async-start | bytes 4194304 | tf_op jit(solution)/shard_map/all_to_all | solution.py:424
  75.4 192.8 %copy-start.4 = (f32[512,512]{1,0:T(8,128)S(1)}, f32[512,512]{1,0:T(8,128)}, u32[]{:S(2)}) copy-start(f32[512,512]{1,0:T(8,128)} %r_ref.3) | copy-start | bytes 3145732
  268.2 3.4 copy-start.1
  406.0 72.9 %all-to-all-start = ((f32[4,4,64,512]{3,2,1,0:T(8,128)}), f32[4,4,64,512]{3,2,1,0:T(8,128)}, u32[]{:S(2)}, u32[]{:S(2)}) async-start(f32[4,4,64,512]{3,2,1,0:T(8,128)} %bitcast.22), calls=%async_computation | async-start | bytes 4194304 | tf_op jit(solution)/shard_map/all_to_all | solution.py:424
  418.2 0.8 copy-start.2
  419.2 1.1 copy-start.3
  420.3 1.2 copy-start.5
  421.5 53.5 %copy-start = (f32[4,4,128,512]{3,2,1,0:T(8,128)S(1)}, f32[4,4,128,512]{3,2,1,0:T(8,128)}, u32[]{:S(2)}) copy-start(f32[4,4,128,512]{3,2,1,0:T(8,128)} %all_to_all.15) | copy-start | bytes 12582916

commit v4 on v3

--- a/solution.py
+++ b/solution.py
@@ -11,7 +11,6 @@
 NB = 128
 HALF = 256
 FIRST = 64
-LAST = 64
 PER_STEP = 4
 
 
@@ -33,28 +32,38 @@
     return a, b
 
 
-def copy_kernel(starts, index_ref, x_ref, *refs):
-    outs, sems = refs[:-1], refs[-1]
-    copies = []
-    for p, (start, o_ref) in enumerate(zip(starts, outs)):
-        for i in range(o_ref.shape[0]):
-            source = x_ref.at[index_ref[i], pl.ds(start, o_ref.shape[1]), :]
-            copies.append(pltpu.make_async_copy(source, o_ref.at[i], sems.at[p, i]))
-    for copy in copies:
-        copy.start()
-    for copy in copies:
-        copy.wait()
-
-
-def gather_rows(index, tiles, spans):
-    count = index.shape[0]
+def copy_kernel(start, index_ref, x_ref, o_ref, held, in_sems, out_sems):
+    count, rows = o_ref.shape[:2]
+
+    def read(i):
+        return pltpu.make_async_copy(x_ref.at[index_ref[i], pl.ds(start, rows), :], held.at[i], in_sems.at[i])
+
+    def write(i):
+        return pltpu.make_async_copy(held.at[i], o_ref.at[i], out_sems.at[i])
+
+    for i in range(count):
+        read(i).start()
+    for i in range(count):
+        read(i).wait()
+        write(i).start()
+    for i in range(count):
+        write(i).wait()
+
+
+def gather_rows(index, tiles, start, rows):
+    shape = (index.shape[0], rows, tiles.shape[2])
     anywhere = pl.BlockSpec(memory_space=pl.ANY)
     return pl.pallas_call(
-        functools.partial(copy_kernel, [start for start, _ in spans]),
+        functools.partial(copy_kernel, start),
         in_specs=[pl.BlockSpec(memory_space=pltpu.SMEM), anywhere],
-        out_specs=[anywhere] * len(spans),
-        out_shape=[jax.ShapeDtypeStruct((count, rows, tiles.shape[2]), tiles.dtype) for _, rows in spans],
-        scratch_shapes=[pltpu.SemaphoreType.DMA((len(spans), count))],
+        out_specs=anywhere,
+        out_shape=jax.ShapeDtypeStruct(shape, tiles.dtype),
+        scratch_shapes=[
+            pltpu.VMEM(shape, tiles.dtype),
+            pltpu.SemaphoreType.DMA((shape[0],)),
+            pltpu.SemaphoreType.DMA((shape[0],)),
+        ],
+        compiler_params=pltpu.CompilerParams(vmem_limit_bytes=24 * 2**20),
         name="gather_rows",
     )(index, tiles)
 
@@ -364,7 +373,7 @@
     o_ref[:, :, HALF:] = b.reshape(shape)
 
 
-def last_product(index, pieces, mh, ml, tile_rows, block, before=None):
+def last_product(index, pieces, mh, ml):
     n = mh.shape[0]
     rows = sum(x.shape[1] for x in pieces)
     whole = pl.BlockSpec((n, n), lambda i, idx: (0, 0))
@@ -374,21 +383,15 @@
 
     operands = [x for _ in range(PER_STEP) for x in pieces] + [mh, ml]
     specs = [tile(x, t) for t in range(PER_STEP) for x in pieces] + [whole, whole]
-    aliases = {}
-    if before is not None:
-        aliases = {1 + len(operands): 0}
-        operands.append(before)
-        specs.append(pl.BlockSpec(memory_space=pl.ANY))
     return pl.pallas_call(
         functools.partial(last_kernel, len(pieces)),
         grid_spec=pltpu.PrefetchScalarGridSpec(
             num_scalar_prefetch=1,
             grid=(OWN_TILES // PER_STEP,),
             in_specs=specs,
-            out_specs=pl.BlockSpec((PER_STEP, rows, n), lambda i, idx: (i, block, 0)),
-        ),
-        out_shape=jax.ShapeDtypeStruct((OWN_TILES, tile_rows, n), jnp.float32),
-        input_output_aliases=aliases,
+            out_specs=pl.BlockSpec((PER_STEP, rows, n), lambda i, idx: (i, 0, 0)),
+        ),
+        out_shape=jax.ShapeDtypeStruct((OWN_TILES, rows, n), jnp.float32),
         compiler_params=pltpu.CompilerParams(vmem_limit_bytes=40 * 2**20),
         cost_estimate=pl.CostEstimate(
             flops=6 * OWN_TILES * rows * n * n, bytes_accessed=8 * OWN_TILES * rows * n, transcendentals=0
@@ -425,11 +428,9 @@
             outgoing.reshape(scenes, pair_most, rows, n), "scene", split_axis=0, concat_axis=0, tiled=True
         ).reshape(capacity, rows, n)
 
-    first, count = lax.optimization_barrier((gather_rows(chosen, observations, [(0, FIRST)])[0], tile_count))
+    first, count = lax.optimization_barrier((gather_rows(chosen, observations, 0, FIRST), tile_count))
     first = exchange(first)
-    middle, rest = gather_rows(
-        chosen, observations, [(FIRST, tile_rows - FIRST - LAST), (tile_rows - LAST, LAST)]
-    )
+    rest = gather_rows(chosen, observations, FIRST, tile_rows - FIRST)
 
     me = lax.axis_index("scene")
     note = jnp.where(is_live, (tile_owner * pair_most + rank) * OWN_TILES + tile_slot, -1)
@@ -438,8 +439,7 @@
     gram = local_gram(count, observations, inverse_factor, chunk * devices)
     rows = lax.axis_size("rows")
     part_sum, notes = sum_part(gram, note, scenes, rows)
-    middle, rest, part_sum = lax.optimization_barrier((middle, rest, part_sum))
-    middle = exchange(middle)
+    rest, part_sum = lax.optimization_barrier((rest, part_sum))
     rest = exchange(rest)
     gram = spread(part_sum, rows)
     notes = notes[:, 0, :capacity]
@@ -450,8 +450,7 @@
     order = jnp.where(match, place[None], 0).sum((1, 2))
 
     factor, mh, ml = factorise(gram, inverse_factor, devices * OWN_TILES * tile_rows)
-    most = last_product(order, [first, middle], mh, ml, tile_rows, 0)
-    return last_product(order, [rest], mh, ml, tile_rows, tile_rows // LAST - 1, most), factor
+    return last_product(order, [first, rest], mh, ml), factor
 
 
 def solution(mesh):

time: 483 us -> 223 us (0.46)
  Pallas kernels: 364 us -> 121 us
  blocking collectives: 97.5 us -> 0 us
  waiting for transfers between devices: 0.01 us -> 72.6 us
  local copies, waits for them, and re-layouts: 6.53 us -> 13.8 us
    pallas_call x2, Pallas kernels: 258 us -> 13.2 us  [gather_rows(): pl.pallas_call(functools.partial(copy_kernel, start), in_specs=[pl.BlockS...]
    all_to_all x1 -> x0, blocking collectives: 97.5 us -> none  [exchange(): lax.all_to_all(outgoing.reshape(scenes, pair_most, rows, n), 'scene', spl...]
    all_to_all x2, waiting for transfers between devices: 0.01 us -> 72.6 us  [exchange(): lax.all_to_all(outgoing.reshape(scenes, pair_most, rows, n), 'scene', spl...]
    unnamed x12 -> x18, local copies, waits for them, and re-layouts: 6.53 us -> 13.8 us
    pallas_call x1, Pallas kernels: 29.8 us -> 34.7 us  [sum_part(): pl.pallas_call(functools.partial(sum_kernel, scenes, rows), out_shape=[ja...]
  transfers between devices with their start and end apart: 2 -> 2, of which waited for: 0 -> 1; matrix products, arithmetic and copies ran while one was open for 0% -> 0% of each run, Pallas kernels for 61% -> 49%
where the time goes in v4:
time: 223 us
  Pallas kernels  121 us (54%)
  waiting for transfers between devices  72.6 us (33%)
  local copies, waits for them, and re-layouts  13.8 us (6%)
  starting transfers between devices  11.7 us (5%)
    all_to_all x2, waiting for transfers between devices, exchange(): lax.all_to_all(outgoing.reshape(scenes, pair_most, rows, n), 'scene', spl...  72.6 us
    pallas_call x1, Pallas kernels, factorise(): pl.pallas_call(functools.partial(factor_kernel, rows_all), out_shape=[jax...  53.5 us
    pallas_call x1, Pallas kernels, sum_part(): pl.pallas_call(functools.partial(sum_kernel, scenes, rows), out_shape=[ja...  34.7 us
    unnamed x18, local copies, waits for them, and re-layouts  13.8 us
    pallas_call x2, Pallas kernels, gather_rows(): pl.pallas_call(functools.partial(copy_kernel, start), in_specs=[pl.BlockS...  13.2 us
    all_to_all x2, starting transfers between devices, exchange(): lax.all_to_all(outgoing.reshape(scenes, pair_most, rows, n), 'scene', spl...  11.7 us
    pallas_call x1, Pallas kernels, spread(): pl.pallas_call(functools.partial(spread_kernel, rows), out_shape=jax.Shap...  7.79 us
    pallas_call x1, Pallas kernels, last_product(): pl.pallas_call(functools.partial(last_kernel, len(pieces)), grid_spec=plt...  6.13 us
  transfers between devices with their start and end apart: 2, of which 1 were waited for; matrix products, arithmetic and copies ran while one was open for 0% of the time, Pallas kernels for 49%

profile of v4, /device:TPU:0, one launch (start us, length us, event | category | flops | bytes accessed | tf_op | source)
XLA Modules:
  0.0 222.8 jit_solution(9721985771065981141)
XLA Ops:
  1.3 0.9 convert_reduce_fusion
  2.2 0.7 select_bitcast_fusion
  2.9 0.1 select_reduce_fusion.1.index_ref
  3.0 0.0 copy-start
  3.0 3.4 %copy-done = f32[16,256,512]{2,1,0:T(8,128)S(1)} copy-done((f32[16,256,512]{2,1,0:T(8,128)S(1)}, f32[16,256,512]{2,1,0:T(8,128)}, u32[]{:S(2)}) %copy-start) | copy-done | bytes 8388632
  6.4 6.3 %gather_rows.2 = f32[16,64,512]{2,1,0:T(8,128)S(1)} custom-call(s32[16]{0:T(128)S(1)} %select_reduce_fusion.1.index_ref, f32[16,256,512]{2,1,0:T(8,128)S(1)} %copy-done), custom_call_target="tpu_custom_call" | custom-call | tf_op jit(solution)/shard_map/gather_rows/pallas_call | solution.py:56
  12.7 0.0 copy-start.4
  12.7 1.3 copy-done.4
  14.0 6.3 %all-to-all-start = ((f32[4,4,64,512]{3,2,1,0:T(8,128)}), f32[4,4,64,512]{3,2,1,0:T(8,128)S(1)}, u32[]{:S(2)}, u32[]{:S(2)}) async-start(f32[4,4,64,512]{3,2,1,0:T(8,128)} %bitcast.15), calls=%async_computation | async-start | bytes 4194304 | tf_op jit(solution)/shard_map/all_to_all | solution.py:427
  20.4 0.0 copy-start.1
  20.4 3.4 %copy-done.1 = f32[16,256,512]{2,1,0:T(8,128)S(1)} copy-done((f32[16,256,512]{2,1,0:T(8,128)S(1)}, f32[16,256,512]{2,1,0:T(8,128)}, u32[]{:S(2)}) %copy-start.1) | copy-done | bytes 8388632
  23.7 0.0 copy-start.2
  23.7 0.0 copy-start.7
  23.7 6.9 %gather_rows.3 = f32[16,192,512]{2,1,0:T(8,128)S(1)} custom-call(s32[16]{0:T(128)S(1)} %select_reduce_fusion.1.index_ref, f32[16,256,512]{2,1,0:T(8,128)S(1)} %copy-done.1), custom_call_target="tpu_custom_call" | custom-call | tf_op jit(solution)/shard_map/gather_rows/pallas_call | solution.py:56
  30.6 0.0 copy-start.3
  30.7 2.6 %copy-done.3 = f32[16,192,512]{2,1,0:T(8,128)} copy-done((f32[16,192,512]{2,1,0:T(8,128)}, f32[16,192,512]{2,1,0:T(8,128)S(1)}, u32[]{:S(2)}) %copy-start.3) | copy-done | bytes 6291480
  33.3 0.0 copy-done.2
  33.3 0.0 copy-done.7
  33.3 6.1 %local_gram.1.g_ref = f32[1280,128]{1,0:T(8,128)S(1)} custom-call(s32[1]{0:T(128)} %copy.7.count_ref, f32[16,256,512]{2,1,0:T(8,128)S(1)} %copy-done.2, f32[512,512]{1,0:T(8,128)S(1)} %copy-done.7), custom_call_target="tpu_custom_call" | custom-call | flops 8589934592 | bytes 8388608 | tf_op jit(solution)/shard_map/local_gram/pallas_call | solution.py:115
  39.3 34.7 %sum_part.1 = (f32[160,128]{1,0:T(8,128)S(1)}, s32[4,8,128]{2,1,0:T(8,128)S(1)}) custom-call(f32[1280,128]{1,0:T(8,128)S(1)} %local_gram.1.g_ref, s32[8,128]{1,0:T(8,128)S(1)} %scatter.4.note_ref), custom_call_target="tpu_custom_call" | custom-call | flops 1638400 | bytes 2621440 | tf_op jit(solution)/shard_map/sum_part/pallas_call | solution.py:216
  74.1 0.0 all-to-all-done
  74.1 5.4 %all-to-all-start.1 = ((f32[4,4,192,512]{3,2,1,0:T(8,128)}), f32[4,4,192,512]{3,2,1,0:T(8,128)}, u32[]{:S(2)}, u32[]{:S(2)}) async-start(f32[4,4,192,512]{3,2,1,0:T(8,128)} %bitcast.14), calls=%async_computation.1 | async-start | bytes 12582912 | tf_op jit(solution)/shard_map/all_to_all | solution.py:427
  79.5 7.8 %spread.1.g_ref = f32[1280,128]{1,0:T(8,128)S(1)} custom-call(f32[160,128]{1,0:T(8,128)S(1)} %get-tuple-element.28.h_ref), custom_call_target="tpu_custom_call" | custom-call | flops 163840 | bytes 1310720 | tf_op jit(solution)/shard_map/spread/pallas_call | solution.py:262
  87.4 0.1 add_select_fusion.1
  87.5 0.1 select_reduce_fusion.index_ref
  87.6 0.0 copy-start.8
  87.6 1.2 copy-done.8
  88.8 53.5 %factorise.1 = (f32[512,512]{1,0:T(8,128)}, bf16[512,512]{1,0:T(8,128)(2,1)S(1)}, bf16[512,512]{1,0:T(8,128)(2,1)S(1)}) custom-call(f32[1280,128]{1,0:T(8,128)S(1)} %spread.1.g_ref, f32[512,512]{1,0:T(8,128)S(1)} %copy-done.8), custom_call_target="tpu_custom_call" | custom-call | flops 5368709120 | bytes 4194304 | tf_op jit(solution)/shard_map/factorise/pallas_call | solution.py:350
  142.3 0.0 copy-start.5
  142.3 0.8 copy-done.5
  143.1 72.6 %all-to-all-done.1 = f32[4,4,192,512]{3,2,1,0:T(8,128)} async-done(((f32[4,4,192,512]{3,2,1,0:T(8,128)}), f32[4,4,192,512]{3,2,1,0:T(8,128)}, u32[]{:S(2)}, u32[]{:S(2)}) %all-to-all-start.1) | async-done | bytes 6291488 | tf_op jit(solution)/shard_map/all_to_all | solution.py:427
  215.6 0.0 copy-start.6
  215.6 1.0 copy-done.6
  216.7 6.1 %last_product.1 = f32[8,256,512]{2,1,0:T(8,128)} custom-call(s32[8]{0:T(128)S(1)} %select_reduce_fusion.index_ref, f32[16,64,512]{2,1,0:T(8,128)S(1)} %bitcast.10, f32[16,192,512]{2,1,0:T(8,128)} %bitcast.6.refs_1_.refs_3_.refs_5_.refs_7_, f32[16,64,512]{2,1,0:T(8,128)S(1)} %bitcast.11, f32[16,192,512]{2,1,0:T(8,128)} %bitcast.6.refs_1_.refs_3_.refs_5_.refs_7_, ...), custom_call_target="tpu_custom_call" | custom-call | flops 3221225472 | bytes 8388608 | tf_op jit(solution)/shard_map/last_product/pallas_call | solution.py:386
  (5 shorter events, 0.0 us)
Async XLA Ops:
  3.0 3.4 %copy-start = (f32[16,256,512]{2,1,0:T(8,128)S(1)}, f32[16,256,512]{2,1,0:T(8,128)}, u32[]{:S(2)}) copy-start(f32[16,256,512]{2,1,0:T(8,128)} %x_ref.5) | copy-start | bytes 25165828
  12.7 1.3 copy-start.4
  14.0 60.1 %all-to-all-start = ((f32[4,4,64,512]{3,2,1,0:T(8,128)}), f32[4,4,64,512]{3,2,1,0:T(8,128)S(1)}, u32[]{:S(2)}, u32[]{:S(2)}) async-start(f32[4,4,64,512]{3,2,1,0:T(8,128)} %bitcast.15), calls=%async_computation | async-start | bytes 4194304 | tf_op jit(solution)/shard_map/all_to_all | solution.py:427
  20.4 3.4 %copy-start.1 = (f32[16,256,512]{2,1,0:T(8,128)S(1)}, f32[16,256,512]{2,1,0:T(8,128)}, u32[]{:S(2)}) copy-start(f32[16,256,512]{2,1,0:T(8,128)} %x_ref.5) | copy-start | bytes 25165828
  23.7 9.5 %copy-start.2 = (f32[16,256,512]{2,1,0:T(8,128)S(1)}, f32[16,256,512]{2,1,0:T(8,128)}, u32[]{:S(2)}) copy-start(f32[16,256,512]{2,1,0:T(8,128)} %x_ref.5) | copy-start | bytes 25165828
  23.7 9.5 %copy-start.7 = (f32[512,512]{1,0:T(8,128)S(1)}, f32[512,512]{1,0:T(8,128)}, u32[]{:S(2)}) copy-start(f32[512,512]{1,0:T(8,128)} %r_ref.3) | copy-start | bytes 3145732
  30.6 2.6 %copy-start.3 = (f32[16,192,512]{2,1,0:T(8,128)}, f32[16,192,512]{2,1,0:T(8,128)S(1)}, u32[]{:S(2)}) copy-start(f32[16,192,512]{2,1,0:T(8,128)S(1)} %gather_rows.3) | copy-start | bytes 18874372
  74.1 141.5 %all-to-all-start.1 = ((f32[4,4,192,512]{3,2,1,0:T(8,128)}), f32[4,4,192,512]{3,2,1,0:T(8,128)}, u32[]{:S(2)}, u32[]{:S(2)}) async-start(f32[4,4,192,512]{3,2,1,0:T(8,128)} %bitcast.14), calls=%async_computation.1 | async-start | bytes 12582912 | tf_op jit(solution)/shard_map/all_to_all | solution.py:427
  87.6 1.2 copy-start.8
  142.3 0.8 copy-start.5
  215.6 1.0 copy-start.6

commit v5 on v4

--- a/solution.py
+++ b/solution.py
@@ -63,7 +63,7 @@
             pltpu.SemaphoreType.DMA((shape[0],)),
             pltpu.SemaphoreType.DMA((shape[0],)),
         ],
-        compiler_params=pltpu.CompilerParams(vmem_limit_bytes=24 * 2**20),
+        compiler_params=pltpu.CompilerParams(vmem_limit_bytes=60 * 2**20),
         name="gather_rows",
     )(index, tiles)
 
@@ -132,7 +132,7 @@
             ],
         ),
         out_shape=jax.ShapeDtypeStruct((packed, NB), jnp.float32),
-        compiler_params=pltpu.CompilerParams(vmem_limit_bytes=40 * 2**20),
+        compiler_params=pltpu.CompilerParams(vmem_limit_bytes=60 * 2**20),
         cost_estimate=pl.CostEstimate(
             flops=8 * capacity * rows * n * n, bytes_accessed=4 * capacity * rows * n, transcendentals=0
         ),

time: 223 us -> 218 us (0.978)
  local copies, waits for them, and re-layouts: 13.8 us -> 4.15 us
  Pallas kernels: 121 us -> 125 us
    unnamed x18 -> x8, local copies, waits for them, and re-layouts: 13.8 us -> 4.14 us
    pallas_call x1, Pallas kernels: 34.7 us -> 39.9 us  [sum_part(): pl.pallas_call(functools.partial(sum_kernel, scenes, rows), out_shape=[ja...]
  transfers between devices with their start and end apart: 2 -> 2, of which waited for: 1 -> 1; matrix products, arithmetic and copies ran while one was open for 0% -> 0% of each run, Pallas kernels for 49% -> 53%
where the time goes in v5:
time: 218 us; the launch traced here: 217 us
  Pallas kernels  125 us (57%)
  waiting for transfers between devices  73.6 us (34%)
  starting transfers between devices  11 us (5%)
  local copies, waits for them, and re-layouts  4.15 us (2%)
  other arithmetic  2.45 us (1%)
    all_to_all x2, waiting for transfers between devices, exchange(): lax.all_to_all(outgoing.reshape(scenes, pair_most, rows, n), 'scene', spl...  73.6 us
    pallas_call x1, Pallas kernels, factorise(): pl.pallas_call(functools.partial(factor_kernel, rows_all), out_shape=[jax...  53.5 us
    pallas_call x1, Pallas kernels, sum_part(): pl.pallas_call(functools.partial(sum_kernel, scenes, rows), out_shape=[ja...  39.9 us
    pallas_call x2, Pallas kernels, gather_rows(): pl.pallas_call(functools.partial(copy_kernel, start), in_specs=[pl.BlockS...  12.4 us
    all_to_all x2, starting transfers between devices, exchange(): lax.all_to_all(outgoing.reshape(scenes, pair_most, rows, n), 'scene', spl...  11 us
    pallas_call x1, Pallas kernels, spread(): pl.pallas_call(functools.partial(spread_kernel, rows), out_shape=jax.Shap...  7.6 us
    pallas_call x1, Pallas kernels, last_product(): pl.pallas_call(functools.partial(last_kernel, len(pieces)), grid_spec=plt...  6.13 us
    pallas_call x1, Pallas kernels, local_gram(): pl.pallas_call(gram_kernel, grid_spec=pltpu.PrefetchScalarGridSpec(num_sc...  5.32 us
  transfers between devices with their start and end apart: 2, of which 1 were waited for; matrix products, arithmetic and copies ran while one was open for 0% of the time, Pallas kernels for 53%

profile of v5, /device:TPU:0, one launch (start us, length us, event | category | flops | bytes accessed | tf_op | source)
XLA Modules:
  0.0 217.4 jit_solution(53555891047474015)
XLA Ops:
  1.3 0.9 convert_reduce_fusion
  2.2 0.7 select_bitcast_fusion
  2.9 0.6 select_reduce_fusion.1.index_ref
  3.5 4.4 %gather_rows.2 = f32[16,64,512]{2,1,0:T(8,128)} custom-call(s32[16]{0:T(128)} %select_reduce_fusion.1.index_ref, f32[16,256,512]{2,1,0:T(8,128)} %x_ref.5), custom_call_target="tpu_custom_call" | custom-call | tf_op jit(solution)/shard_map/gather_rows/pallas_call | solution.py:56
  7.9 5.7 %all-to-all-start = ((f32[4,4,64,512]{3,2,1,0:T(8,128)}), f32[4,4,64,512]{3,2,1,0:T(8,128)S(1)}, u32[]{:S(2)}, u32[]{:S(2)}) async-start(f32[4,4,64,512]{3,2,1,0:T(8,128)} %bitcast.15), calls=%async_computation | async-start | bytes 4194304 | tf_op jit(solution)/shard_map/all_to_all | solution.py:427
  13.7 7.9 %gather_rows.3 = f32[16,192,512]{2,1,0:T(8,128)} custom-call(s32[16]{0:T(128)} %select_reduce_fusion.1.index_ref, f32[16,256,512]{2,1,0:T(8,128)} %x_ref.5), custom_call_target="tpu_custom_call" | custom-call | tf_op jit(solution)/shard_map/gather_rows/pallas_call | solution.py:56
  21.6 5.3 %local_gram.1.g_ref = f32[1280,128]{1,0:T(8,128)} custom-call(s32[1]{0:T(128)} %copy.7.count_ref, f32[16,256,512]{2,1,0:T(8,128)} %x_ref.5, f32[512,512]{1,0:T(8,128)} %r_ref.3), custom_call_target="tpu_custom_call" | custom-call | flops 8589934592 | bytes 8388608 | tf_op jit(solution)/shard_map/local_gram/pallas_call | solution.py:115
  27.0 0.0 copy-start
  27.0 1.1 copy-done
  28.0 39.9 %sum_part.1 = (f32[160,128]{1,0:T(8,128)S(1)}, s32[4,8,128]{2,1,0:T(8,128)S(1)}) custom-call(f32[1280,128]{1,0:T(8,128)S(1)} %copy-done, s32[8,128]{1,0:T(8,128)S(1)} %scatter.4.note_ref), custom_call_target="tpu_custom_call" | custom-call | flops 1638400 | bytes 2621440 | tf_op jit(solution)/shard_map/sum_part/pallas_call | solution.py:216
  68.0 0.0 all-to-all-done
  68.0 5.2 %all-to-all-start.1 = ((f32[4,4,192,512]{3,2,1,0:T(8,128)}), f32[4,4,192,512]{3,2,1,0:T(8,128)}, u32[]{:S(2)}, u32[]{:S(2)}) async-start(f32[4,4,192,512]{3,2,1,0:T(8,128)} %bitcast.14), calls=%async_computation.1 | async-start | bytes 12582912 | tf_op jit(solution)/shard_map/all_to_all | solution.py:427
  73.2 7.6 %spread.1.g_ref = f32[1280,128]{1,0:T(8,128)S(1)} custom-call(f32[160,128]{1,0:T(8,128)S(1)} %get-tuple-element.28.h_ref), custom_call_target="tpu_custom_call" | custom-call | flops 163840 | bytes 1310720 | tf_op jit(solution)/shard_map/spread/pallas_call | solution.py:262
  80.9 0.1 add_select_fusion.1
  81.0 0.1 select_reduce_fusion.index_ref
  81.1 0.0 copy-start.3
  81.1 1.2 copy-done.3
  82.3 53.5 %factorise.1 = (f32[512,512]{1,0:T(8,128)}, bf16[512,512]{1,0:T(8,128)(2,1)S(1)}, bf16[512,512]{1,0:T(8,128)(2,1)S(1)}) custom-call(f32[1280,128]{1,0:T(8,128)S(1)} %spread.1.g_ref, f32[512,512]{1,0:T(8,128)S(1)} %copy-done.3), custom_call_target="tpu_custom_call" | custom-call | flops 5368709120 | bytes 4194304 | tf_op jit(solution)/shard_map/factorise/pallas_call | solution.py:350
  135.8 0.0 copy-start.1
  135.8 0.8 copy-done.1
  136.6 73.6 %all-to-all-done.1 = f32[4,4,192,512]{3,2,1,0:T(8,128)} async-done(((f32[4,4,192,512]{3,2,1,0:T(8,128)}), f32[4,4,192,512]{3,2,1,0:T(8,128)}, u32[]{:S(2)}, u32[]{:S(2)}) %all-to-all-start.1) | async-done | bytes 6291488 | tf_op jit(solution)/shard_map/all_to_all | solution.py:427
  210.2 0.0 copy-start.2
  210.2 1.0 copy-done.2
  211.2 6.1 %last_product.1 = f32[8,256,512]{2,1,0:T(8,128)} custom-call(s32[8]{0:T(128)S(1)} %select_reduce_fusion.index_ref, f32[16,64,512]{2,1,0:T(8,128)S(1)} %bitcast.10, f32[16,192,512]{2,1,0:T(8,128)} %bitcast.6.refs_1_.refs_3_.refs_5_.refs_7_, f32[16,64,512]{2,1,0:T(8,128)S(1)} %bitcast.11, f32[16,192,512]{2,1,0:T(8,128)} %bitcast.6.refs_1_.refs_3_.refs_5_.refs_7_, ...), custom_call_target="tpu_custom_call" | custom-call | flops 3221225472 | bytes 8388608 | tf_op jit(solution)/shard_map/last_product/pallas_call | solution.py:386
  (5 shorter events, 0.0 us)
Async XLA Ops:
  7.9 60.0 %all-to-all-start = ((f32[4,4,64,512]{3,2,1,0:T(8,128)}), f32[4,4,64,512]{3,2,1,0:T(8,128)S(1)}, u32[]{:S(2)}, u32[]{:S(2)}) async-start(f32[4,4,64,512]{3,2,1,0:T(8,128)} %bitcast.15), calls=%async_computation | async-start | bytes 4194304 | tf_op jit(solution)/shard_map/all_to_all | solution.py:427
  27.0 1.1 copy-start
  68.0 142.2 %all-to-all-start.1 = ((f32[4,4,192,512]{3,2,1,0:T(8,128)}), f32[4,4,192,512]{3,2,1,0:T(8,128)}, u32[]{:S(2)}, u32[]{:S(2)}) async-start(f32[4,4,192,512]{3,2,1,0:T(8,128)} %bitcast.14), calls=%async_computation.1 | async-start | bytes 12582912 | tf_op jit(solution)/shard_map/all_to_all | solution.py:427
  81.1 1.2 copy-start.3
  135.8 0.8 copy-start.1
  210.2 1.0 copy-start.2

commit v6 on v5

--- a/solution.py
+++ b/solution.py
@@ -10,7 +10,7 @@
 OWN_TILES = 8
 NB = 128
 HALF = 256
-FIRST = 64
+FIRST = 48
 PER_STEP = 4
 
 
@@ -172,107 +172,6 @@
     return pl.ds(pl.multiple_of(start, 8), size)
 
 
-def sum_kernel(scenes, rows, g_ref, note_ref, out_ref, notes_ref, h0, h1, rx0, rx1, rx2, ss, rs):
-    packed = g_ref.shape[0]
-    half, part, chunk = packed // 2, packed // rows, packed // rows // scenes
-    mates = rows // 2
-    scene, row, core, mate = place()
-    pair = (scene, row + 1 - 2 * core)
-    plane = [(scene, lax.rem(mate + d, mates) * 2 + core) for d in range(1, mates)]
-    line = [(lax.rem(scene + d, scenes), row) for d in range(1, scenes)]
-    greet([pair] + plane + line)
-    send = sender(ss, rs)
-
-    copy = send(g_ref.at[span((1 - core) * half, half)], rx0, pair)
-    copy.wait()
-    h0[...] = g_ref[span(core * half, half), :] + rx0[...]
-
-    copies = [send(h0.at[span(lax.div(p[1], 2) * part, part)], rx1.at[d], p) for d, p in enumerate(plane)]
-    total = h0[span(mate * part, part), :]
-    for d, copy in enumerate(copies):
-        copy.wait()
-        total += rx1[d]
-    h1[...] = total
-
-    copies = [send(h1.at[span(p[0] * chunk, chunk)], rx2.at[d], p) for d, p in enumerate(line)]
-    notes = [send(note_ref, notes_ref.at[scene], p) for p in line]
-    notes_ref[scene] = note_ref[...]
-    total = h1[span(scene * chunk, chunk), :]
-    for d, copy in enumerate(copies):
-        copy.wait()
-        total += rx2[d]
-
-    own = span(scene * chunk, chunk)
-    out_ref[own, :] = total
-    for copy in [send(out_ref.at[own], out_ref.at[own], p) for p in line] + notes:
-        copy.wait()
-
-
-def sum_part(gram, note, scenes, rows):
-    packed = gram.shape[0]
-    half, part, chunk = packed // 2, packed // rows, packed // rows // scenes
-    copies = rows // 2 + 3 * (scenes - 1)
-    whole = pl.BlockSpec(memory_space=pltpu.VMEM)
-    return pl.pallas_call(
-        functools.partial(sum_kernel, scenes, rows),
-        out_shape=[
-            jax.ShapeDtypeStruct((part, NB), gram.dtype),
-            jax.ShapeDtypeStruct((scenes,) + note.shape, note.dtype),
-        ],
-        in_specs=[whole, whole],
-        out_specs=[whole, whole],
-        scratch_shapes=[
-            pltpu.VMEM((half, NB), jnp.float32),
-            pltpu.VMEM((part, NB), jnp.float32),
-            pltpu.VMEM((half, NB), jnp.float32),
-            pltpu.VMEM((rows // 2 - 1, part, NB), jnp.float32),
-            pltpu.VMEM((scenes - 1, chunk, NB), jnp.float32),
-            pltpu.SemaphoreType.DMA((copies,)),
-            pltpu.SemaphoreType.DMA((copies,)),
-        ],
-        compiler_params=pltpu.CompilerParams(
-            collective_id=0, has_side_effects=True, vmem_limit_bytes=24 * 2**20
-        ),
-        cost_estimate=pl.CostEstimate(flops=10 * packed * NB, bytes_accessed=16 * packed * NB, transcendentals=0),
-        name="sum_part",
-    )(gram, note)
-
-
-def spread_kernel(rows, h_ref, out_ref, ss, rs):
-    packed = out_ref.shape[0]
-    half, part = packed // 2, packed // rows
-    mates = rows // 2
-    scene, row, core, mate = place()
-    pair = (scene, row + 1 - 2 * core)
-    plane = [(scene, lax.rem(mate + d, mates) * 2 + core) for d in range(1, mates)]
-    greet([pair] + plane)
-    send = sender(ss, rs)
-    own = span(core * half + mate * part, part)
-    copies = [send(h_ref, out_ref.at[own], p) for p in plane]
-    out_ref[own, :] = h_ref[...]
-    for copy in copies:
-        copy.wait()
-    own = span(core * half, half)
-    send(out_ref.at[own], out_ref.at[own], pair).wait()
-
-
-def spread(part_sum, rows):
-    whole = pl.BlockSpec(memory_space=pltpu.VMEM)
-    packed = part_sum.shape[0] * rows
-    return pl.pallas_call(
-        functools.partial(spread_kernel, rows),
-        out_shape=jax.ShapeDtypeStruct((packed, NB), part_sum.dtype),
-        in_specs=[whole],
-        out_specs=whole,
-        scratch_shapes=[pltpu.SemaphoreType.DMA((rows // 2,)), pltpu.SemaphoreType.DMA((rows // 2,))],
-        compiler_params=pltpu.CompilerParams(
-            collective_id=1, has_side_effects=True, vmem_limit_bytes=24 * 2**20
-        ),
-        cost_estimate=pl.CostEstimate(flops=packed * NB, bytes_accessed=8 * packed * NB, transcendentals=0),
-        name="spread",
-    )(part_sum)
-
-
 def eliminate(block):
     lane = lax.broadcasted_iota(jnp.int32, (8, NB), 1)
     sub = lax.broadcasted_iota(jnp.int32, (8, 1), 0)
@@ -345,22 +244,111 @@
     ml_ref[...] = l
 
 
-def factorise(gram, inverse_factor, rows_all):
+def heart_kernel(
+    scenes, rows, rows_all, g_ref, note_ref, r_ref, rest_ref,
+    u_ref, mh_ref, ml_ref, notes_ref, received_ref,
+    h0, h1, rx0, rx1, rx2, part_sum, gram, work, kept, ss, rs, ls,
+):
+    packed = g_ref.shape[0]
+    half, part, chunk = packed // 2, packed // rows, packed // rows // scenes
+    mates = rows // 2
+    pair_most = rest_ref.shape[0] // scenes
+    scene, row, core, mate = place()
+    pair = (scene, row + 1 - 2 * core)
+    plane = [(scene, lax.rem(mate + d, mates) * 2 + core) for d in range(1, mates)]
+    line = [(lax.rem(scene + d, scenes), row) for d in range(1, scenes)]
+    greet([pair] + plane + line)
+    send = sender(ss, rs)
+    seat = pl.ds(scene * pair_most, pair_most)
+    own_in = pltpu.make_async_copy(rest_ref.at[seat], kept, ls.at[0])
+    own_out = pltpu.make_async_copy(kept, received_ref.at[seat], ls.at[1])
+    own_in.start()
+
+    copy = send(g_ref.at[span((1 - core) * half, half)], rx0, pair)
+    copy.wait()
+    h0[...] = g_ref[span(core * half, half), :] + rx0[...]
+
+    copies = [send(h0.at[span(lax.div(p[1], 2) * part, part)], rx1.at[d], p) for d, p in enumerate(plane)]
+    total = h0[span(mate * part, part), :]
+    for d, copy in enumerate(copies):
+        copy.wait()
+        total += rx1[d]
+    h1[...] = total
+
+    copies = [send(h1.at[span(p[0] * chunk, chunk)], rx2.at[d], p) for d, p in enumerate(line)]
+    notes = [send(note_ref, notes_ref.at[scene], p) for p in line]
+    notes_ref[scene] = note_ref[...]
+    total = h1[span(scene * chunk, chunk), :]
+    for d, copy in enumerate(copies):
+        copy.wait()
+        total += rx2[d]
+    own = span(scene * chunk, chunk)
+    part_sum[own, :] = total
+    copies = [send(part_sum.at[own], part_sum.at[own], p) for p in line] + notes
+
+    exchange = []
+    for m in range(scenes - 1, 0, -1):
+        other = 0
+        for bit in range(scenes.bit_length() - 1):
+            have = lax.rem(lax.div(scene, 2**bit), 2)
+            other += 2**bit * (1 - have if m >> bit & 1 else have)
+        exchange.append(send(rest_ref.at[pl.ds(other * pair_most, pair_most)], received_ref.at[seat], (other, row)))
+    for copy in copies:
+        copy.wait()
+
+    own = span(core * half + mate * part, part)
+    copies = [send(part_sum, gram.at[own], p) for p in plane]
+    gram[own, :] = part_sum[...]
+    for copy in copies:
+        copy.wait()
+    own = span(core * half, half)
+    send(gram.at[own], gram.at[own], pair).wait()
+    own_in.wait()
+    own_out.start()
+
+    factor_kernel(rows_all, gram, r_ref, u_ref, mh_ref, ml_ref, work)
+    own_out.wait()
+    for copy in exchange:
+        copy.wait()
+
+
+def heart(gram, note, inverse_factor, rest, scenes, rows, rows_all):
+    packed = gram.shape[0]
     n = inverse_factor.shape[0]
+    half, part, chunk = packed // 2, packed // rows, packed // rows // scenes
+    copies = rows + 4 * (scenes - 1)
+    whole = pl.BlockSpec(memory_space=pltpu.VMEM)
+    anywhere = pl.BlockSpec(memory_space=pl.ANY)
     return pl.pallas_call(
-        functools.partial(factor_kernel, rows_all),
+        functools.partial(heart_kernel, scenes, rows, rows_all),
         out_shape=[
             jax.ShapeDtypeStruct((n, n), jnp.float32),
             jax.ShapeDtypeStruct((n, n), jnp.bfloat16),
             jax.ShapeDtypeStruct((n, n), jnp.bfloat16),
+            jax.ShapeDtypeStruct((scenes,) + note.shape, note.dtype),
+            jax.ShapeDtypeStruct(rest.shape, rest.dtype),
         ],
-        in_specs=[pl.BlockSpec(memory_space=pltpu.VMEM)] * 2,
-        out_specs=[pl.BlockSpec(memory_space=pltpu.VMEM)] * 3,
-        scratch_shapes=[pltpu.VMEM((n, 2 * n), jnp.float32)],
-        compiler_params=pltpu.CompilerParams(vmem_limit_bytes=40 * 2**20),
-        cost_estimate=pl.CostEstimate(flops=40 * n**3, bytes_accessed=16 * n * n, transcendentals=0),
-        name="factorise",
-    )(gram, inverse_factor)
+        in_specs=[whole, whole, whole, anywhere],
+        out_specs=[whole, whole, whole, whole, anywhere],
+        scratch_shapes=[
+            pltpu.VMEM((half, NB), jnp.float32),
+            pltpu.VMEM((part, NB), jnp.float32),
+            pltpu.VMEM((half, NB), jnp.float32),
+            pltpu.VMEM((rows // 2 - 1, part, NB), jnp.float32),
+            pltpu.VMEM((scenes - 1, chunk, NB), jnp.float32),
+            pltpu.VMEM((part, NB), jnp.float32),
+            pltpu.VMEM((packed, NB), jnp.float32),
+            pltpu.VMEM((n, 2 * n), jnp.float32),
+            pltpu.VMEM((rest.shape[0] // scenes,) + rest.shape[1:], jnp.float32),
+            pltpu.SemaphoreType.DMA((copies,)),
+            pltpu.SemaphoreType.DMA((copies,)),
+            pltpu.SemaphoreType.DMA((2,)),
+        ],
+        compiler_params=pltpu.CompilerParams(
+            collective_id=0, has_side_effects=True, vmem_limit_bytes=60 * 2**20
+        ),
+        name="heart",
+    )(gram, note, inverse_factor, rest)
 
 
 def last_kernel(pieces, index_ref, *refs):
@@ -438,10 +426,9 @@
     chunk = -(-len(lower_blocks(n)) * NB // devices // 8) * 8
     gram = local_gram(count, observations, inverse_factor, chunk * devices)
     rows = lax.axis_size("rows")
-    part_sum, notes = sum_part(gram, note, scenes, rows)
-    rest, part_sum = lax.optimization_barrier((rest, part_sum))
-    rest = exchange(rest)
-    gram = spread(part_sum, rows)
+    factor, mh, ml, notes, rest = heart(
+        gram, note, inverse_factor, rest, scenes, rows, devices * OWN_TILES * tile_rows
+    )
     notes = notes[:, 0, :capacity]
     seat = notes // OWN_TILES
     mine = (notes >= 0) & (seat // pair_most == me)
@@ -449,7 +436,6 @@
     match = mine[None] & ((notes % OWN_TILES)[None] == jnp.arange(OWN_TILES, dtype=jnp.int32)[:, None, None])
     order = jnp.where(match, place[None], 0).sum((1, 2))
 
-    factor, mh, ml = factorise(gram, inverse_factor, devices * OWN_TILES * tile_rows)
     return last_product(order, [first, rest], mh, ml), factor
 
 

time: 218 us -> 220 us (level)
  Pallas kernels: 125 us -> 200 us
  waiting for transfers between devices: 73.6 us -> 0.01 us
  starting transfers between devices: 11 us -> 7.66 us
  local copies, waits for them, and re-layouts: 4.15 us -> 7.3 us
    all_to_all x2 -> x1, waiting for transfers between devices: 73.6 us -> 0.01 us  [exchange(): lax.all_to_all(outgoing.reshape(scenes, pair_most, rows, n), 'scene', spl...]
    pallas_call x3 -> x1, Pallas kernels: 101 us -> 166 us  [heart(): pl.pallas_call(functools.partial(heart_kernel, scenes, rows, rows_all), o...]
    pallas_call x1, Pallas kernels: 5.32 us -> 19.6 us  [local_gram(): pl.pallas_call(gram_kernel, grid_spec=pltpu.PrefetchScalarGridSpec(num_sc...]
    all_to_all x2 -> x1, starting transfers between devices: 11 us -> 7.66 us  [exchange(): lax.all_to_all(outgoing.reshape(scenes, pair_most, rows, n), 'scene', spl...]
    pallas_call x2, Pallas kernels: 12.4 us -> 9.41 us  [gather_rows(): pl.pallas_call(functools.partial(copy_kernel, start), in_specs=[pl.BlockS...]
    unnamed x8 -> x9, local copies, waits for them, and re-layouts: 4.14 us -> 5.99 us
  transfers between devices with their start and end apart: 2 -> 1, of which waited for: 1 -> 0; matrix products, arithmetic and copies ran while one was open for 0% -> 1% of each run, Pallas kernels for 53% -> 88%
where the time goes in v6:
time: 220 us; the launch traced here: 219 us
  Pallas kernels  200 us (91%)
  starting transfers between devices  7.66 us (3%)
  local copies, waits for them, and re-layouts  7.3 us (3%)
  other arithmetic  2.44 us (1%)
    pallas_call x1, Pallas kernels, heart(): pl.pallas_call(functools.partial(heart_kernel, scenes, rows, rows_all), o...  166 us
    pallas_call x1, Pallas kernels, local_gram(): pl.pallas_call(gram_kernel, grid_spec=pltpu.PrefetchScalarGridSpec(num_sc...  19.6 us
    pallas_call x2, Pallas kernels, gather_rows(): pl.pallas_call(functools.partial(copy_kernel, start), in_specs=[pl.BlockS...  9.41 us
    all_to_all x1, starting transfers between devices, exchange(): lax.all_to_all(outgoing.reshape(scenes, pair_most, rows, n), 'scene', spl...  7.66 us
    unnamed x9, local copies, waits for them, and re-layouts  5.99 us
    pallas_call x1, Pallas kernels, last_product(): pl.pallas_call(functools.partial(last_kernel, len(pieces)), grid_spec=plt...  4.71 us
  transfers between devices with their start and end apart: 1, of which 0 were waited for; matrix products, arithmetic and copies ran while one was open for 1% of the time, Pallas kernels for 88%

profile of v6, /device:TPU:0, one launch (start us, length us, event | category | flops | bytes accessed | tf_op | source)
XLA Modules:
  0.0 218.7 jit_solution(18191063426960265750)
XLA Ops:
  1.3 0.9 convert_reduce_fusion
  2.2 0.7 select_bitcast_fusion
  2.9 0.6 select_reduce_fusion.1.index_ref
  3.5 3.1 %gather_rows.2 = f32[16,48,512]{2,1,0:T(8,128)} custom-call(s32[16]{0:T(128)} %select_reduce_fusion.1.index_ref, f32[16,256,512]{2,1,0:T(8,128)} %x_ref.5), custom_call_target="tpu_custom_call" | custom-call | tf_op jit(solution)/shard_map/gather_rows/pallas_call | solution.py:56
  6.6 7.7 %all-to-all-start = ((f32[4,4,48,512]{3,2,1,0:T(8,128)}), f32[4,4,48,512]{3,2,1,0:T(8,128)S(1)}, u32[]{:S(2)}, u32[]{:S(2)}) async-start(f32[4,4,48,512]{3,2,1,0:T(8,128)} %bitcast.12), calls=%async_computation | async-start | bytes 3145728 | tf_op jit(solution)/shard_map/all_to_all | solution.py:415
  14.2 6.4 %gather_rows.3.rest_ref = f32[16,208,512]{2,1,0:T(8,128)} custom-call(s32[16]{0:T(128)} %select_reduce_fusion.1.index_ref, f32[16,256,512]{2,1,0:T(8,128)} %x_ref.5), custom_call_target="tpu_custom_call" | custom-call | tf_op jit(solution)/shard_map/gather_rows/pallas_call | solution.py:56
  20.6 0.6 scatter.4.note_ref
  21.2 19.6 %local_gram.1.g_ref = f32[1280,128]{1,0:T(8,128)} custom-call(s32[1]{0:T(128)} %copy.8.count_ref, f32[16,256,512]{2,1,0:T(8,128)} %x_ref.5, f32[512,512]{1,0:T(8,128)} %r_ref.3), custom_call_target="tpu_custom_call" | custom-call | flops 8589934592 | bytes 8388608 | tf_op jit(solution)/shard_map/local_gram/pallas_call | solution.py:115
  40.8 166.2 %heart.1 = (f32[512,512]{1,0:T(8,128)}, bf16[512,512]{1,0:T(8,128)(2,1)}, bf16[512,512]{1,0:T(8,128)(2,1)}, s32[4,8,128]{2,1,0:T(8,128)}, f32[16,208,512]{2,1,0:T(8,128)}) custom-call(f32[1280,128]{1,0:T(8,128)} %local_gram.1.g_ref, s32[8,128]{1,0:T(8,128)} %scatter.4.note_ref, f32[512,512]{1,0:T(8,128)} %r_ref.3, f32[16,208,512]{2,1,0:T(8,128)} %gather_rows.3.rest_ref), custom_call_target="tpu_custom_call" | custom-call | tf_op jit(solution)/shard_map/heart/pallas_call | solution.py:322
  207.0 0.7 slice.19
  207.8 0.1 add_select_fusion.1
  207.8 0.1 select_reduce_fusion.index_ref
  208.0 0.0 all-to-all-done
  208.0 0.0 copy-start
  208.0 2.9 %copy-done = f32[16,208,512]{2,1,0:T(8,128)S(1)} copy-done((f32[16,208,512]{2,1,0:T(8,128)S(1)}, f32[16,208,512]{2,1,0:T(8,128)}, u32[]{:S(2)}) %copy-start) | copy-done | bytes 6815768
  210.9 0.0 copy-start.1
  210.9 1.0 copy-done.1
  211.9 0.0 copy-start.2
  212.0 1.0 copy-done.2
  213.0 0.0 copy-start.3
  213.0 4.7 %last_product.1 = f32[8,256,512]{2,1,0:T(8,128)} custom-call(s32[8]{0:T(128)S(1)} %select_reduce_fusion.index_ref, f32[16,48,512]{2,1,0:T(8,128)S(1)} %bitcast.8, f32[16,208,512]{2,1,0:T(8,128)S(1)} %copy-done, f32[16,48,512]{2,1,0:T(8,128)S(1)} %bitcast.9, f32[16,208,512]{2,1,0:T(8,128)S(1)} %copy-done, f32[16,48,512]{2,1,0:T(8,128)S(1)} %bitcast.10, ...), custom_call_target="tpu_custom_call" | custom-call | flops 3221225472 | bytes 8388608 | tf_op jit(solution)/shard_map/last_product/pallas_call | solution.py:374
  217.7 0.0 copy-done.3
  217.7 1.0 copy.9
  (3 shorter events, 0.0 us)
Async XLA Ops:
  6.6 201.4 %all-to-all-start = ((f32[4,4,48,512]{3,2,1,0:T(8,128)}), f32[4,4,48,512]{3,2,1,0:T(8,128)S(1)}, u32[]{:S(2)}, u32[]{:S(2)}) async-start(f32[4,4,48,512]{3,2,1,0:T(8,128)} %bitcast.12), calls=%async_computation | async-start | bytes 3145728 | tf_op jit(solution)/shard_map/all_to_all | solution.py:415
  208.0 2.9 %copy-start = (f32[16,208,512]{2,1,0:T(8,128)S(1)}, f32[16,208,512]{2,1,0:T(8,128)}, u32[]{:S(2)}) copy-start(f32[16,208,512]{2,1,0:T(8,128)} %get-tuple-element.24.refs_1_.refs_3_.refs_5_.refs_7_) | copy-start | bytes 20447236
  210.9 1.0 copy-start.1
  211.9 1.0 copy-start.2
  213.0 4.7 %copy-start.3 = (f32[512,512]{1,0:T(8,128)S(1)}, f32[512,512]{1,0:T(8,128)}, u32[]{:S(2)}) copy-start(f32[512,512]{1,0:T(8,128)} %get-tuple-element.35) | copy-start | bytes 3145732

commit v7 on v6

--- a/solution.py
+++ b/solution.py
@@ -10,7 +10,7 @@
 OWN_TILES = 8
 NB = 128
 HALF = 256
-FIRST = 48
+FIRST = 64
 PER_STEP = 4
 
 
@@ -380,7 +380,7 @@
             out_specs=pl.BlockSpec((PER_STEP, rows, n), lambda i, idx: (i, 0, 0)),
         ),
         out_shape=jax.ShapeDtypeStruct((OWN_TILES, rows, n), jnp.float32),
-        compiler_params=pltpu.CompilerParams(vmem_limit_bytes=40 * 2**20),
+        compiler_params=pltpu.CompilerParams(vmem_limit_bytes=60 * 2**20),
         cost_estimate=pl.CostEstimate(
             flops=6 * OWN_TILES * rows * n * n, bytes_accessed=8 * OWN_TILES * rows * n, transcendentals=0
         ),

time: 220 us -> 214 us (0.973)
  local copies, waits for them, and re-layouts: 7.3 us -> 3.65 us
    pallas_call x1, Pallas kernels: 19.6 us -> 13.5 us  [local_gram(): pl.pallas_call(gram_kernel, grid_spec=pltpu.PrefetchScalarGridSpec(num_sc...]
    unnamed x9 -> x5, local copies, waits for them, and re-layouts: 5.99 us -> 2.33 us
    pallas_call x1, Pallas kernels: 4.71 us -> 7.33 us  [last_product(): pl.pallas_call(functools.partial(last_kernel, len(pieces)), grid_spec=plt...]
where the time goes in v7:
time: 214 us; the launch traced here: 213 us
  Pallas kernels  198 us (93%)
  starting transfers between devices  6.89 us (3%)
  local copies, waits for them, and re-layouts  3.65 us (2%)
  other arithmetic  2.95 us (1%)
    pallas_call x1, Pallas kernels, heart(): pl.pallas_call(functools.partial(heart_kernel, scenes, rows, rows_all), o...  167 us
    pallas_call x1, Pallas kernels, local_gram(): pl.pallas_call(gram_kernel, grid_spec=pltpu.PrefetchScalarGridSpec(num_sc...  13.5 us
    pallas_call x2, Pallas kernels, gather_rows(): pl.pallas_call(functools.partial(copy_kernel, start), in_specs=[pl.BlockS...  10.1 us
    pallas_call x1, Pallas kernels, last_product(): pl.pallas_call(functools.partial(last_kernel, len(pieces)), grid_spec=plt...  7.33 us
    all_to_all x1, starting transfers between devices, exchange(): lax.all_to_all(outgoing.reshape(scenes, pair_most, rows, n), 'scene', spl...  6.89 us
  transfers between devices with their start and end apart: 1, of which 0 were waited for; matrix products, arithmetic and copies ran while one was open for 1% of the time, Pallas kernels for 88%

profile of v7, /device:TPU:0, one launch (start us, length us, event | category | flops | bytes accessed | tf_op | source)
XLA Modules:
  0.0 213.0 jit_solution(3590540962782319647)
XLA Ops:
  1.3 0.9 convert_reduce_fusion
  2.2 0.7 select_bitcast_fusion
  2.9 0.6 select_reduce_fusion.1.index_ref
  3.5 3.8 %gather_rows.2 = f32[16,64,512]{2,1,0:T(8,128)} custom-call(s32[16]{0:T(128)} %select_reduce_fusion.1.index_ref, f32[16,256,512]{2,1,0:T(8,128)} %x_ref.5), custom_call_target="tpu_custom_call" | custom-call | tf_op jit(solution)/shard_map/gather_rows/pallas_call | solution.py:56
  7.3 6.9 %all-to-all-start = ((f32[4,4,64,512]{3,2,1,0:T(8,128)}), f32[4,4,64,512]{3,2,1,0:T(8,128)S(1)}, u32[]{:S(2)}, u32[]{:S(2)}) async-start(f32[4,4,64,512]{3,2,1,0:T(8,128)} %bitcast.12), calls=%async_computation | async-start | bytes 4194304 | tf_op jit(solution)/shard_map/all_to_all | solution.py:415
  14.2 6.4 %gather_rows.3.rest_ref = f32[16,192,512]{2,1,0:T(8,128)} custom-call(s32[16]{0:T(128)} %select_reduce_fusion.1.index_ref, f32[16,256,512]{2,1,0:T(8,128)} %x_ref.5), custom_call_target="tpu_custom_call" | custom-call | tf_op jit(solution)/shard_map/gather_rows/pallas_call | solution.py:56
  20.6 0.6 scatter.4.note_ref
  21.2 13.5 %local_gram.1.g_ref = f32[1280,128]{1,0:T(8,128)} custom-call(s32[1]{0:T(128)} %copy.8.count_ref, f32[16,256,512]{2,1,0:T(8,128)} %x_ref.5, f32[512,512]{1,0:T(8,128)} %r_ref.3), custom_call_target="tpu_custom_call" | custom-call | flops 8589934592 | bytes 8388608 | tf_op jit(solution)/shard_map/local_gram/pallas_call | solution.py:115
  34.7 167.2 %heart.1 = (f32[512,512]{1,0:T(8,128)}, bf16[512,512]{1,0:T(8,128)(2,1)}, bf16[512,512]{1,0:T(8,128)(2,1)}, s32[4,8,128]{2,1,0:T(8,128)}, f32[16,192,512]{2,1,0:T(8,128)}) custom-call(f32[1280,128]{1,0:T(8,128)} %local_gram.1.g_ref, s32[8,128]{1,0:T(8,128)} %scatter.4.note_ref, f32[512,512]{1,0:T(8,128)} %r_ref.3, f32[16,192,512]{2,1,0:T(8,128)} %gather_rows.3.rest_ref), custom_call_target="tpu_custom_call" | custom-call | tf_op jit(solution)/shard_map/heart/pallas_call | solution.py:322
  201.8 0.7 slice.19
  202.6 0.1 add_select_fusion.1
  202.7 0.6 select_reduce_fusion.index_ref
  203.3 0.0 all-to-all-done
  203.3 0.0 copy-start
  203.3 1.4 copy-done
  204.6 0.0 copy-start.1
  204.6 7.3 %last_product.1 = f32[8,256,512]{2,1,0:T(8,128)} custom-call(s32[8]{0:T(128)} %select_reduce_fusion.index_ref, f32[16,64,512]{2,1,0:T(8,128)} %bitcast.8, f32[16,192,512]{2,1,0:T(8,128)} %get-tuple-element.24.refs_1_.refs_3_.refs_5_.refs_7_, f32[16,64,512]{2,1,0:T(8,128)} %bitcast.9, f32[16,192,512]{2,1,0:T(8,128)} %get-tuple-element.24.refs_1_.refs_3_.refs_5_.refs_7_, ...), custom_call_target="tpu_custom_call" | custom-call | flops 3221225472 | bytes 8388608 | tf_op jit(solution)/shard_map/last_product/pallas_call | solution.py:374
  212.0 0.0 copy-done.1
  212.0 1.0 copy.9
  (3 shorter events, 0.0 us)
Async XLA Ops:
  7.3 196.0 %all-to-all-start = ((f32[4,4,64,512]{3,2,1,0:T(8,128)}), f32[4,4,64,512]{3,2,1,0:T(8,128)S(1)}, u32[]{:S(2)}, u32[]{:S(2)}) async-start(f32[4,4,64,512]{3,2,1,0:T(8,128)} %bitcast.12), calls=%async_computation | async-start | bytes 4194304 | tf_op jit(solution)/shard_map/all_to_all | solution.py:415
  203.3 1.4 copy-start
  204.6 7.3 %copy-start.1 = (f32[512,512]{1,0:T(8,128)S(1)}, f32[512,512]{1,0:T(8,128)}, u32[]{:S(2)}) copy-start(f32[512,512]{1,0:T(8,128)} %get-tuple-element.35) | copy-start | bytes 3145732
